TPU v7x, 32 devices: a whole 2x2x4 slice. The times are simulated.
32 devices in a mesh: tm: 4 (over z), chan: 8 (over y, x, core).
Axes of the slice: x: 2, y: 2, z: 4, core: 2. Of those that a mesh axis runs over, the one named last changes fastest.
Arguments:
- signal: float32 [256, 8192], P('chan', 'tm'), may hold values from -6 to 6
- band: float32 [2, 16, 256], replicated, may hold values from -4 to 4
- response: float32 [2, 4, 16, 2048], P(None, 'tm', None, 'chan'), may hold values from -6 to 6
- offsets: int32 [4, 2048], P('tm', 'chan'), may hold values from 0 to 255, as said below
Outputs:
- smoothed: float32 [256, 8192], P('chan', 'tm')
Inputs may be any that keep to these rules, and one draw needn't show every extreme that they name: Row c of bin k's gain holds the columns c + offsets + j, wrapping around the 256 channels; every offset lies within 8 of 0 modulo 256, and entry [p, q] is the same for all p and for all q in one run of 64 consecutive q.
All inputs are finite; a program needn't handle non-finite values.
Results may differ from a plain program's by a relative error of at most 0.0003.
Values sent between devices are 32-bit elements; how exact they have to be, the bound alone decides.
A program may use at most 64 MiB of HBM per device.

v0:
```python
import math

import jax
import jax.numpy as jnp
from jax import lax
from jax.sharding import PartitionSpec as P

PRECISE = lax.Precision.HIGHEST


def from_partner(block, axis, stride):
    count = lax.axis_size(axis)
    route = []
    for low in range(count):
        high = low | 1 << stride
        if high != low and high < count:
            route += [(low, high), (high, low)]
    return lax.ppermute(block, axis, route)


def twiddle(numer, length):
    angle = -2.0 * math.pi / length * numer.astype(jnp.float32)
    return (jnp.cos(angle), jnp.sin(angle))


def dft_table(length):
    steps = lax.iota(jnp.int32, length)
    return twiddle(steps[:, None] * steps[None, :] % length, length)


def reverse_bits(value, bit_count):
    result = value * 0
    for bit_index in range(bit_count):
        result = result + value // (1 << bit_index) % 2 * (1 << bit_count - 1 - bit_index)
    return result


def complex_einsum(form, left_real, left_imag, right_real, right_imag):
    out_real = jnp.einsum(form, left_real, right_real, precision=PRECISE) - jnp.einsum(
        form, left_imag, right_imag, precision=PRECISE
    )
    out_imag = jnp.einsum(form, left_real, right_imag, precision=PRECISE) + jnp.einsum(
        form, left_imag, right_real, precision=PRECISE
    )
    return (out_real, out_imag)


def forward_local(real_part, imag_part, phase_bin, total_len, inner_len):
    channel_count, length = real_part.shape
    outer_len = length // inner_len
    sample_pos = lax.iota(jnp.int32, length)
    cosine, sine_part = twiddle(sample_pos * phase_bin % total_len, total_len)
    real_part, imag_part = (
        real_part * cosine - imag_part * sine_part,
        real_part * sine_part + imag_part * cosine,
    )
    real_part = real_part.reshape(channel_count, inner_len, outer_len)
    imag_part = imag_part.reshape(channel_count, inner_len, outer_len)
    table_real, table_imag = dft_table(inner_len)
    real_part, imag_part = complex_einsum(
        "cab,ak->cbk", real_part, imag_part, table_real, table_imag
    )
    outer_ids = lax.iota(jnp.int32, outer_len)[:, None]
    inner_ids = lax.iota(jnp.int32, inner_len)[None, :]
    cosine, sine_part = twiddle(outer_ids * inner_ids, length)
    real_part, imag_part = (
        real_part * cosine - imag_part * sine_part,
        real_part * sine_part + imag_part * cosine,
    )
    table_real, table_imag = dft_table(outer_len)
    return complex_einsum("cbk,bm->mck", real_part, imag_part, table_real, table_imag)


def inverse_local(spec_real, spec_imag, phase_bin, total_len):
    outer_len, channel_count, inner_len = spec_real.shape
    length = outer_len * inner_len
    table_real, table_imag = dft_table(outer_len)
    real_part, imag_part = complex_einsum(
        "mck,mb->cbk", spec_real, spec_imag, table_real, -table_imag
    )
    outer_ids = lax.iota(jnp.int32, outer_len)[:, None]
    inner_ids = lax.iota(jnp.int32, inner_len)[None, :]
    cosine, sine_part = twiddle(outer_ids * inner_ids, length)
    sine_part = -sine_part
    real_part, imag_part = (
        real_part * cosine - imag_part * sine_part,
        real_part * sine_part + imag_part * cosine,
    )
    table_real, table_imag = dft_table(inner_len)
    real_part, imag_part = complex_einsum(
        "cbk,ka->cab", real_part, imag_part, table_real, -table_imag
    )
    real_part = real_part.reshape(channel_count, length)
    imag_part = imag_part.reshape(channel_count, length)
    sample_pos = lax.iota(jnp.int32, length)
    cosine, sine_part = twiddle(sample_pos * phase_bin % total_len, total_len)
    sine_part = -sine_part
    return (real_part * cosine - imag_part * sine_part, real_part * sine_part + imag_part * cosine)


def mix_bins(spread, band, response, offsets):
    fine_len, channel_all, inner_len = (spread.shape[1], spread.shape[2], spread.shape[3])
    band_width = band.shape[1]
    half_width = band_width // 2
    shift_cols = offsets.reshape(1, fine_len, 1, inner_len)
    centered = (shift_cols + half_width) % channel_all - half_width
    moved = jnp.zeros_like(spread)
    for shift_amount in range(-half_width, half_width + 1):
        rolled = jnp.roll(spread, -shift_amount, axis=2)
        moved = jnp.where(centered == shift_amount, rolled, moved)
    moved_real = moved[0]
    moved_imag = moved[1]
    wide_real = jnp.concatenate([moved_real, moved_real[:, : band_width - 1]], axis=1)
    wide_imag = jnp.concatenate([moved_imag, moved_imag[:, : band_width - 1]], axis=1)
    responses = response.reshape(2, band_width, fine_len, 1, inner_len)
    acc_real = jnp.zeros_like(moved_real)
    acc_imag = jnp.zeros_like(moved_imag)
    for lag_index in range(band_width):
        value_real = wide_real[:, lag_index : lag_index + channel_all]
        value_imag = wide_imag[:, lag_index : lag_index + channel_all]
        gain_real = band[0, lag_index][None, :, None]
        gain_imag = band[1, lag_index][None, :, None]
        coef_real = gain_real * responses[0, lag_index] - gain_imag * responses[1, lag_index]
        coef_imag = gain_real * responses[1, lag_index] + gain_imag * responses[0, lag_index]
        acc_real = acc_real + coef_real * value_real - coef_imag * value_imag
        acc_imag = acc_imag + coef_real * value_imag + coef_imag * value_real
    return (acc_real, acc_imag)


def per_device(signal, band, response, offsets):
    blocks = lax.axis_size("tm")
    levels = blocks.bit_length() - 1
    device_pos = lax.axis_index("tm")
    phase_bin = reverse_bits(device_pos, levels)
    channel_count, length = signal.shape
    total_len = length * blocks
    inner_len = math.gcd(128, length // lax.axis_size("chan"))
    real_part = signal
    imag_part = jnp.zeros_like(signal)
    for bit_index in range(levels - 1, -1, -1):
        half_span = 1 << bit_index
        partner = from_partner(jnp.stack([real_part, imag_part]), "tm", bit_index)
        upper_half = device_pos // half_span % 2 == 1
        cosine, sine_part = twiddle(device_pos % half_span, 2 * half_span)
        diff_real = partner[0] - real_part
        diff_imag = partner[1] - imag_part
        new_real = jnp.where(
            upper_half, diff_real * cosine - diff_imag * sine_part, real_part + partner[0]
        )
        new_imag = jnp.where(
            upper_half, diff_real * sine_part + diff_imag * cosine, imag_part + partner[1]
        )
        real_part, imag_part = (new_real, new_imag)
    spec_real, spec_imag = forward_local(real_part, imag_part, phase_bin, total_len, inner_len)
    spread = lax.all_to_all(
        jnp.stack([spec_real, spec_imag]), "chan", split_axis=1, concat_axis=2, tiled=True
    )
    mixed_real, mixed_imag = mix_bins(spread, band, response, offsets)
    returned = lax.all_to_all(
        jnp.stack([mixed_real, mixed_imag]), "chan", split_axis=2, concat_axis=1, tiled=True
    )
    real_part, imag_part = inverse_local(returned[0], returned[1], phase_bin, total_len)
    for bit_index in range(levels):
        half_span = 1 << bit_index
        partner = from_partner(jnp.stack([real_part, imag_part]), "tm", bit_index)
        upper_half = device_pos // half_span % 2 == 1
        cosine, sine_part = twiddle(device_pos % half_span, 2 * half_span)
        sine_part = -sine_part
        base_real = jnp.where(upper_half, partner[0], real_part)
        base_imag = jnp.where(upper_half, partner[1], imag_part)
        scaled_real = jnp.where(upper_half, real_part, partner[0])
        scaled_imag = jnp.where(upper_half, imag_part, partner[1])
        prod_real = scaled_real * cosine - scaled_imag * sine_part
        prod_imag = scaled_real * sine_part + scaled_imag * cosine
        real_part = jnp.where(upper_half, base_real - prod_real, base_real + prod_real)
        imag_part = jnp.where(upper_half, base_imag - prod_imag, base_imag + prod_imag)
    smoothed = real_part / total_len
    return smoothed


def solution(mesh):
    in_specs = (P("chan", "tm"), P(), P(None, "tm", None, "chan"), P("tm", "chan"))
    out_specs = P("chan", "tm")
    return jax.shard_map(
        per_device, mesh=mesh, in_specs=in_specs, out_specs=out_specs, check_vma=False
    )
```

profile of v0, /device:TPU:27, one launch (start us, length us, event | category | flops | bytes accessed | tf_op | source)
XLA Modules:
  0.0 131.5 jit_solution(9396679975925223463)
XLA Ops:
  0.0 1.1 stack.44
  1.1 0.1 collective-permute-start
  1.4 0.6 copy-done.1
  2.0 0.6 copy-done.3
  2.7 24.3 %collective-permute-done = f32[2,32,2048]{2,1,0:T(8,128)S(1)} collective-permute-done((f32[2,32,2048]{2,1,0:T(8,128)S(1)}, f32[2,32,2048]{2,1,0:T(8,128)S(1)}, u32[]{:S(2)}, u32[]{:S(2)}) %collective-permute-start) | collective-permute-done | bytes 524320 | tf_op jit(solution)/shard_map/ppermute | solution.py:18
  27.0 0.1 add_select_fusion.4
  27.1 0.1 collective-permute-start.1
  27.2 0.1 fusion.101
  27.3 12.9 %collective-permute-done.1 = f32[2,32,2048]{2,1,0:T(8,128)S(1)} collective-permute-done((f32[2,32,2048]{2,1,0:T(8,128)S(1)}, f32[2,32,2048]{2,1,0:T(8,128)S(1)}, u32[]{:S(2)}, u32[]{:S(2)}) %collective-permute-start.1) | collective-permute-done | bytes 524320 | tf_op jit(solution)/shard_map/ppermute | solution.py:18
  40.2 0.1 multiply_add_fusion.18
  40.4 0.3 copy.200
  40.7 0.5 copy.201
  41.2 0.6 fusion.58
  41.8 0.6 fusion.52
  42.4 0.3 copy.202
  42.8 0.5 copy.203
  43.3 0.6 convolution_subtract_fusion.3
  43.9 0.6 convolution_add_fusion.3
  44.5 0.4 fusion.46
  44.9 0.4 fusion.45
  45.4 0.4 fusion.3
  45.8 0.4 fusion.2
  46.2 0.9 copy.206
  47.2 5.4 %all-to-all-start = ((f32[2,16,32,128]{3,2,0,1:T(8,128)}), f32[2,16,32,128]{3,2,0,1:T(8,128)S(1)}, u32[]{:S(2)}, u32[]{:S(2)}) async-start(f32[2,16,32,128]{3,2,0,1:T(8,128)} %copy.206), calls=%async_computation | async-start | bytes 1048576 | tf_op jit(solution)/shard_map/all_to_all | solution.py:155
  52.6 8.1 %all-to-all-done = f32[2,16,32,128]{3,2,0,1:T(8,128)S(1)} async-done(((f32[2,16,32,128]{3,2,0,1:T(8,128)}), f32[2,16,32,128]{3,2,0,1:T(8,128)S(1)}, u32[]{:S(2)}, u32[]{:S(2)}) %all-to-all-start) | async-done | bytes 524320 | tf_op jit(solution)/shard_map/all_to_all | solution.py:155
  60.8 0.1 fusion.186
  60.9 0.1 fusion.188
  61.0 0.1 fusion.190
  61.0 0.1 fusion.192
  61.1 0.1 fusion.194
  61.2 0.1 fusion.196
  61.3 0.1 fusion.198
  61.4 0.1 fusion.184
  61.5 1.4 %maximum_select_fusion = f32[2,2,256,128]{3,2,1,0:T(8,128)S(1)} fusion(f32[2,2,8,128]{3,2,1,0:T(8,128)S(1)} %get-tuple-element.23, f32[2,2,248,128]{3,2,1,0:T(8,128)S(1)} %get-tuple-element.25, f32[2,2,7,128]{3,2,1,0:T(8,128)S(1)} %get-tuple-element.27, f32[2,2,249,128]{3,2,1,0:T(8,128)S(1)} %get-tuple-element.29, ...), kind=kLoop, calls=%fused_computation.42 | loop fusion | flops 4325376 | bytes 9441536 | tf_op jit(solution)/shard_map/jit(_where)/select_n | solution.py:110
  63.0 3.3 %subtract_bitcast_fusion.1 = f32[1,2,256,128]{3,2,1,0:T(8,128)S(1)} fusion(f32[2,256,128]{2,1,0:T(8,128)S(1)} %get-tuple-element.20, f32[2,256,128]{2,1,0:T(8,128)S(1)} %get-tuple-element.21, f32[2,15,128]{2,1,0:T(8,128)S(1)} %slice.675, f32[2,15,128]{2,1,0:T(8,128)S(1)} %slice.678, f32[2,128]{1,0:T(2,128)S(1)} %get-tuple-element.74, f32[256]{0:T(256)S(1)} %bitcast.379, ...), kind=kLoop, calls=%fused_computation.115 | loop fusion | flops 12386304 | bytes 882688 | tf_op jit(solution)/shard_map/stack | solution.py:160
  66.4 3.3 %add_bitcast_fusion.1 = f32[1,2,256,128]{3,2,1,0:T(8,128)S(1)} fusion(f32[2,256,128]{2,1,0:T(8,128)S(1)} %get-tuple-element.21, f32[2,256,128]{2,1,0:T(8,128)S(1)} %get-tuple-element.20, f32[2,15,128]{2,1,0:T(8,128)S(1)} %slice.675, f32[2,15,128]{2,1,0:T(8,128)S(1)} %slice.678, f32[2,128]{1,0:T(2,128)S(1)} %get-tuple-element.74, f32[256]{0:T(256)S(1)} %bitcast.380, ...), kind=kLoop, calls=%fused_computation.114 | loop fusion | flops 12386304 | bytes 882688 | tf_op jit(solution)/shard_map/stack | solution.py:160
  69.7 1.2 copy.239
  70.9 4.9 %all-to-all-start.1 = ((f32[2,2,256,128]{3,1,0,2:T(2,128)}), f32[2,2,256,128]{3,1,0,2:T(2,128)S(1)}, u32[]{:S(2)}, u32[]{:S(2)}) async-start(f32[2,2,256,128]{3,1,0,2:T(2,128)} %copy.239), calls=%async_computation.1 | async-start | bytes 1048576 | tf_op jit(solution)/shard_map/all_to_all | solution.py:159
  75.8 0.1 fusion.113
  75.9 0.1 fusion.114
  76.0 8.1 %all-to-all-done.1 = f32[2,2,256,128]{3,1,0,2:T(2,128)S(1)} async-done(((f32[2,2,256,128]{3,1,0,2:T(2,128)}), f32[2,2,256,128]{3,1,0,2:T(2,128)S(1)}, u32[]{:S(2)}, u32[]{:S(2)}) %all-to-all-start.1) | async-done | bytes 524320 | tf_op jit(solution)/shard_map/all_to_all | solution.py:159
  84.1 0.2 copy.241
  84.3 0.4 fusion.81
  84.8 0.4 fusion.87
  85.2 0.2 copy.242
  85.4 0.4 convolution_add_fusion.1
  85.8 0.5 add_bitcast_fusion
  86.3 0.6 fusion.43
  86.9 0.6 fusion.41
  87.6 0.6 fusion.1
  88.2 0.5 copy.245
  88.7 0.3 copy.246
  89.0 0.6 fusion
  89.7 0.5 copy.249
  90.2 0.3 copy.250
  90.5 0.1 multiply_subtract_fusion
  90.6 0.1 collective-permute-start.2
  90.7 13.0 %collective-permute-done.2 = f32[2,32,2048]{2,1,0:T(8,128)S(1)} collective-permute-done((f32[2,32,2048]{2,1,0:T(8,128)S(1)}, f32[2,32,2048]{2,1,0:T(8,128)S(1)}, u32[]{:S(2)}, u32[]{:S(2)}) %collective-permute-start.2) | collective-permute-done | bytes 524320 | tf_op jit(solution)/shard_map/ppermute | solution.py:18
  103.7 0.1 add_select_fusion.1
  103.8 0.8 pad_maximum_fusion.4
  104.7 0.3 copy.254
  105.0 0.3 copy.256
  105.3 25.3 %collective-permute-done.3 = f32[2,32,2048]{2,1,0:T(8,128)S(1)} collective-permute-done((f32[2,32,2048]{2,1,0:T(8,128)}, f32[2,32,2048]{2,1,0:T(8,128)S(1)}, u32[]{:S(2)}, u32[]{:S(2)}) %collective-permute-start.3) | collective-permute-done | bytes 524320 | tf_op jit(solution)/shard_map/ppermute | solution.py:18
  130.6 1.0 select_multiply_fusion
  (35 shorter events, 0.6 us)
Async XLA Ops:
  0.0 27.0 %copy-start = (f32[32,2048]{1,0:T(8,128)S(1)}, f32[32,2048]{1,0:T(8,128)}, u32[]{:S(2)}) copy-start(f32[32,2048]{1,0:T(8,128)} %param.4) | copy-start | bytes 786436
  1.1 25.9 %collective-permute-start = (f32[2,32,2048]{2,1,0:T(8,128)S(1)}, f32[2,32,2048]{2,1,0:T(8,128)S(1)}, u32[]{:S(2)}, u32[]{:S(2)}) collective-permute-start(f32[2,32,2048]{2,1,0:T(8,128)S(1)} %stack.44), channel_id=1, source_target_pairs={{0,16},{16,0},{8,24},{24,8},{1,17},{17,1},{9,25},{25,9},{2,18},{18... | collective-permute-start | bytes 1572872 | tf_op jit(solution)/shard_map/ppermute | solution.py:18
  1.2 0.8 copy-start.1
  2.0 0.7 copy-start.3
  27.1 13.1 %collective-permute-start.1 = (f32[2,32,2048]{2,1,0:T(8,128)S(1)}, f32[2,32,2048]{2,1,0:T(8,128)S(1)}, u32[]{:S(2)}, u32[]{:S(2)}) collective-permute-start(f32[2,32,2048]{2,1,0:T(8,128)S(1)} %pad_maximum_fusion), channel_id=1, source_target_pairs={{0,8},{8,0},{16,24},{24,16},{1,9},{9,1},{17,25},{25,17},{2,10},{10... | collective-permute-start | bytes 1572872 | tf_op jit(solution)/shard_map/ppermute | solution.py:18
  47.2 5.4 %copy-start.2 = (f32[2,16,256]{2,1,0:T(8,128)S(1)}, f32[2,16,256]{2,1,0:T(8,128)}, u32[]{:S(2)}) copy-start(f32[2,16,256]{2,1,0:T(8,128)} %param.5) | copy-start | bytes 98308
  47.2 13.6 %all-to-all-start = ((f32[2,16,32,128]{3,2,0,1:T(8,128)}), f32[2,16,32,128]{3,2,0,1:T(8,128)S(1)}, u32[]{:S(2)}, u32[]{:S(2)}) async-start(f32[2,16,32,128]{3,2,0,1:T(8,128)} %copy.206), calls=%async_computation | async-start | bytes 1048576 | tf_op jit(solution)/shard_map/all_to_all | solution.py:155
  70.9 13.2 %all-to-all-start.1 = ((f32[2,2,256,128]{3,1,0,2:T(2,128)}), f32[2,2,256,128]{3,1,0,2:T(2,128)S(1)}, u32[]{:S(2)}, u32[]{:S(2)}) async-start(f32[2,2,256,128]{3,1,0,2:T(2,128)} %copy.239), calls=%async_computation.1 | async-start | bytes 1048576 | tf_op jit(solution)/shard_map/all_to_all | solution.py:159
  90.6 13.1 %collective-permute-start.2 = (f32[2,32,2048]{2,1,0:T(8,128)S(1)}, f32[2,32,2048]{2,1,0:T(8,128)S(1)}, u32[]{:S(2)}, u32[]{:S(2)}) collective-permute-start(f32[2,32,2048]{2,1,0:T(8,128)S(1)} %pad_maximum_fusion.3), channel_id=1, source_target_pairs={{0,8},{8,0},{16,24},{24,16},{1,9},{9,1},{17,25},{25,17},{2,10},{10... | collective-permute-start | bytes 1572872 | tf_op jit(solution)/shard_map/ppermute | solution.py:18
  104.7 25.9 %collective-permute-start.3 = (f32[2,32,2048]{2,1,0:T(8,128)}, f32[2,32,2048]{2,1,0:T(8,128)S(1)}, u32[]{:S(2)}, u32[]{:S(2)}) collective-permute-start(f32[2,32,2048]{2,1,0:T(8,128)} %pad_maximum_fusion.4), channel_id=1, source_target_pairs={{0,16},{16,0},{8,24},{24,8},{1,17},{17,1},{9,25},{25,9},{2,18},{18... | collective-permute-start | bytes 1572872 | tf_op jit(solution)/shard_map/ppermute | solution.py:18
where the time goes:
time: 132 us
  waiting for transfers between devices  91.8 us (70%)
  other arithmetic  10.7 us (8%)
  starting transfers between devices  10.6 us (8%)
  local copies, waits for them, and re-layouts  9.46 us (7%)
  matrix products  8.33 us (6%)
    ppermute x4, waiting for transfers between devices, from_partner(): return lax.ppermute(block, axis, route)  75.6 us
    all_to_all x1, waiting for transfers between devices, per_device(): lax.all_to_all(jnp.stack([spec_real, spec_imag]), 'chan', split_axis=1, c...  8.13 us
    all_to_all x1, waiting for transfers between devices, per_device(): lax.all_to_all(jnp.stack([mixed_real, mixed_imag]), 'chan', split_axis=2,...  8.09 us
    another operation x3, other arithmetic, per_device(): jnp.stack([mixed_real, mixed_imag])  6.63 us
    all_to_all x1, starting transfers between devices, per_device(): lax.all_to_all(jnp.stack([spec_real, spec_imag]), 'chan', split_axis=1, c...  5.37 us
    all_to_all x1, starting transfers between devices, per_device(): lax.all_to_all(jnp.stack([mixed_real, mixed_imag]), 'chan', split_axis=2,...  4.95 us
  transfers between devices with their start and end apart: 6, of which 6 were waited for; matrix products, arithmetic and copies ran while one was open for 1% of the time, Pallas kernels for 0%

commit v1 on v0

--- a/solution.py
+++ b/solution.py
@@ -2,7 +2,10 @@
 
 import jax
 import jax.numpy as jnp
+import numpy as np
 from jax import lax
+from jax.experimental import pallas as pl
+from jax.experimental.pallas import tpu as pltpu
 from jax.sharding import PartitionSpec as P
 
 PRECISE = lax.Precision.HIGHEST
@@ -178,9 +181,272 @@
     return smoothed
 
 
+TM, CHAN, ROWS, LANES, OUTER, BANDW, HALF = 4, 8, 8, 128, 64, 16, 8
+DEVICES = TM * CHAN
+TOTAL = OUTER * LANES
+
+
+def split_hi_lo(value):
+    hi = value.astype(jnp.bfloat16)
+    return hi, (value - hi.astype(jnp.float32)).astype(jnp.bfloat16)
+
+
+def dot3(left, right, dims):
+    (lh, ll), (rh, rl) = left, right
+
+    def one(a, b):
+        return lax.dot_general(a, b, (dims, ((), ())), preferred_element_type=jnp.float32)
+
+    return one(lh, rh) + (one(lh, rl) + one(ll, rh))
+
+
+def outer_table():
+    n1 = np.arange(OUTER)
+    table = np.zeros((OUTER, OUTER))
+    for pair in range(DEVICES):
+        angle = 2 * np.pi * (n1 * pair % OUTER) / OUTER
+        table[2 * pair] = np.cos(angle)
+        table[2 * pair + 1] = -np.sin(angle) if pair else (-1.0) ** n1
+    return table
+
+
+def rev(t):
+    return (t % 2) * 2 + t // 2
+
+
+def fused(signal, resp, band, base, turn, table, out,
+          xin, ybuf, sbuf, rbuf, rt, xp, mv, mm, wh, wl, dbuf, yback, zbuf, rsend, rrecv, send, recv):
+    t, g = lax.axis_index("tm"), lax.axis_index("chan")
+    d = CHAN // 2 * g + rev(t)
+    e = TM * g + t
+
+    def remote(src, dst, k, target):
+        return pltpu.make_async_remote_copy(
+            src_ref=src, dst_ref=dst, send_sem=send.at[k], recv_sem=recv.at[k],
+            device_id=target, device_id_type=pl.DeviceIdType.MESH)
+
+    def local(src, dst, sem):
+        return pltpu.make_async_copy(src, dst, sem)
+
+    for hop in range(1, TM):
+        to = (t + hop) % TM
+        remote(signal.at[pl.ds(ROWS * to, ROWS)], xin.at[:, pl.ds(16 * t, 16)], 0, (to, g)).start()
+    local(signal.at[pl.ds(ROWS * t, ROWS)], xin.at[:, pl.ds(16 * t, 16)], recv.at[0]).start()
+
+    def send_resp(part, s, block, target):
+        return pltpu.make_async_remote_copy(
+            src_ref=resp.at[s], dst_ref=rbuf.at[part, pl.ds(16 * block, 16)], send_sem=rsend.at[part],
+            recv_sem=rrecv.at[part], device_id=target, device_id_type=pl.DeviceIdType.MESH)
+
+    t_b = jnp.where(t < 2, t, 5 - t)
+    s_own = jnp.where(t == 0, (8 - g) % 8, 7 - g) + 8
+    local(resp.at[g], rbuf.at[0, pl.ds(16 * g, 16)], rrecv.at[0]).start()
+    for hop in range(1, CHAN):
+        to = (g + hop) % CHAN
+        send_resp(0, to, g, (t, to)).start()
+        send_resp(1, jnp.where(t == 0, (8 - to) % 8, 7 - to) + 8, g, (t_b, to)).start()
+
+    @pl.when(t < 2)
+    def _():
+        local(resp.at[s_own], rbuf.at[1, pl.ds(16 * g, 16)], rrecv.at[1]).start()
+
+    @pl.when(t >= 2)
+    def _():
+        pltpu.make_async_remote_copy(
+            src_ref=resp.at[s_own], dst_ref=rbuf.at[1, pl.ds(16 * g, 16)], send_sem=rsend.at[2],
+            recv_sem=rrecv.at[1], device_id=(5 - t, g), device_id_type=pl.DeviceIdType.MESH).start()
+
+    first = d == 0
+    for part in range(2):
+        tc, ts = turn[:, 2 * part : 2 * part + 1], turn[:, 2 * part + 1 : 2 * part + 2]
+        bc, bs = base[0], base[1]
+        tr = tc * bc - ts * bs
+        ti = tc * bs + ts * bc
+        zero = jnp.zeros_like(tr)
+        if part == 0:
+            blocks = ((tr, ti), (jnp.where(first, zero, -ti), jnp.where(first, zero, tr)))
+        else:
+            blocks = ((jnp.where(first, zero, tr), jnp.where(first, zero, ti)),
+                      (jnp.where(first, tr, ti), jnp.where(first, ti, -tr)))
+        for row in range(2):
+            for col in range(2):
+                hi, lo = split_hi_lo(blocks[row][col])
+                where = (slice(LANES * row, LANES * (row + 1)),
+                         slice(LANES * (2 * part + col), LANES * (2 * part + col + 1)))
+                wh[where] = hi
+                wl[where] = lo
+
+    local(xin, xin, recv.at[0]).wait()
+    ycols = ybuf.reshape(DEVICES * 2 * ROWS, LANES)
+    for c in range(ROWS):
+        ycols[pl.ds(c, OUTER, stride=ROWS), :] = dot3((table[0], table[1]), split_hi_lo(xin[c]), ((1,), (0,)))
+
+    def send_pair(hop, carry):
+        to = (d + hop) % DEVICES
+        remote(ybuf.at[to], sbuf.at[e], 1, (rev(to % 4), to // 4)).start()
+        return carry
+
+    lax.fori_loop(1, DEVICES, send_pair, 0)
+    local(ybuf.at[d], sbuf.at[e], recv.at[1]).start()
+
+    for part in range(2):
+        local(rbuf.at[part], rbuf.at[part], rrecv.at[part]).wait()
+        rt[part] = rbuf[part].T
+
+    local(sbuf, sbuf, recv.at[1]).wait()
+    rows = jnp.concatenate([sbuf[:, 0].reshape(256, LANES), sbuf[:, 1].reshape(256, LANES)], axis=1)
+    spec = dot3(split_hi_lo(rows), (wh[...], wl[...]), ((1,), (0,)))
+    for part in range(2):
+        for ri in range(2):
+            at = LANES * (2 * part + ri)
+            piece = spec[:, at : at + LANES]
+            xp[part, ri, 8:264] = piece
+            xp[part, ri, 0:8] = piece[248:256]
+            xp[part, ri, 264:288] = piece[0:24]
+
+    def shift(i, carry):
+        at = 8 * i
+        for part in range(2):
+            off = jnp.broadcast_to(rt[part, 32:33, :], (8, LANES))
+            got = [jnp.zeros((8, LANES), jnp.float32)] * 2
+            for o in range(-HALF, HALF + 1):
+                hit = off == float(o)
+                for ri in range(2):
+                    got[ri] = jnp.where(hit, xp[part, ri, pl.ds(at + 8 + o, 8), :], got[ri])
+            for ri in range(2):
+                mv[part, ri, pl.ds(pl.multiple_of(at, 8), 8), :] = got[ri]
+        return carry
+
+    lax.fori_loop(0, 34, shift, 0)
+
+    def chunk(step, carry):
+        top = 64 * ((step + g // 2) % 4)
+
+        def mix(i, inner):
+            at = pl.multiple_of(top + 8 * i, 8)
+            gains = band[pl.ds(at, 8), :]
+            acc = [jnp.zeros((8, LANES), jnp.float32)] * 4
+            for j in range(BANDW):
+                br = jnp.broadcast_to(gains[:, j : j + 1], (8, LANES))
+                bi = jnp.broadcast_to(gains[:, BANDW + j : BANDW + j + 1], (8, LANES))
+                for part in range(2):
+                    rr, ri = rt[part, j : j + 1, :], rt[part, BANDW + j : BANDW + j + 1, :]
+                    cr = br * rr - bi * ri
+                    ci = br * ri + bi * rr
+                    xr = mv[part, 0, pl.ds(at + j, 8), :]
+                    xi = mv[part, 1, pl.ds(at + j, 8), :]
+                    acc[2 * part] = acc[2 * part] + (cr * xr - ci * xi)
+                    acc[2 * part + 1] = acc[2 * part + 1] + (cr * xi + ci * xr)
+            for q in range(4):
+                mm[pl.ds(pl.multiple_of(8 * i, 8), 8), LANES * q : LANES * (q + 1)] = acc[q]
+            return inner
+
+        lax.fori_loop(0, 8, mix, 0)
+        back = dot3(split_hi_lo(mm[...]), (wh[...], wl[...]), ((1,), (1,)))
+        e0 = top // 8
+        for ri in range(2):
+            dbuf[pl.ds(e0, 8), ri] = back[:, LANES * ri : LANES * (ri + 1)].reshape(8, 8, LANES)
+
+        def send_back(u, inner):
+            to = e0 + u
+
+            @pl.when(to != e)
+            def _():
+                remote(dbuf.at[to], yback.at[d], 2, (to % TM, to // TM)).start()
+
+            @pl.when(to == e)
+            def _():
+                local(dbuf.at[to], yback.at[d], recv.at[2]).start()
+
+            return inner
+
+        lax.fori_loop(0, 8, send_back, 0)
+        return carry
+
+    lax.fori_loop(0, 4, chunk, 0)
+
+    local(yback, yback, recv.at[2]).wait()
+    bcols = yback.reshape(DEVICES * 2 * ROWS, LANES)
+    for c in range(ROWS):
+        zbuf[c] = dot3((table[2], table[3]), split_hi_lo(bcols[pl.ds(c, OUTER, stride=ROWS), :]), ((1,), (0,)))
+    for hop in range(1, TM):
+        to = (t + hop) % TM
+        remote(zbuf.at[:, pl.ds(16 * to, 16)], out.at[pl.ds(ROWS * t, ROWS)], 3, (to, g)).start()
+    local(zbuf.at[:, pl.ds(16 * t, 16)], out.at[pl.ds(ROWS * t, ROWS)], recv.at[3]).start()
+    local(out, out, recv.at[3]).wait()
+
+    for k in (0, 3):
+        local(signal.at[pl.ds(0, 24)], signal.at[pl.ds(0, 24)], send.at[k]).wait()
+    for k in (1, 2):
+        local(ybuf.at[pl.ds(0, 31)], ybuf.at[pl.ds(0, 31)], send.at[k]).wait()
+    for part in range(2):
+        local(resp.at[pl.ds(0, 7)], resp.at[pl.ds(0, 7)], rsend.at[part]).wait()
+
+    @pl.when(t >= 2)
+    def _():
+        local(resp.at[0], resp.at[0], rsend.at[2]).wait()
+
+
+def per_device_fused(signal, band, response, offsets):
+    t, g = lax.axis_index("tm"), lax.axis_index("chan")
+    d = CHAN // 2 * g + rev(t)
+    resp = response.reshape(2 * BANDW, 16, 16).transpose(2, 1, 0)
+    centered = ((offsets + HALF) % 256 - HALF).astype(jnp.float32).reshape(1, 16, 16).transpose(2, 1, 0)
+    resp = jnp.pad(jnp.concatenate([resp, centered], axis=2), ((0, 0), (0, 0), (0, LANES - 2 * BANDW - 1)))
+    gains = band.reshape(2 * BANDW, 256).T
+
+    n2 = np.arange(LANES)
+    angle = -2 * np.pi * (n2[:, None] * n2[None, :] % LANES) / LANES
+    base = jnp.asarray(np.stack([np.cos(angle), np.sin(angle)]).astype(np.float32))
+    pairs = np.arange(DEVICES)[:, None]
+    other = np.where(pairs == 0, DEVICES, OUTER - pairs)
+    turns = [-2 * np.pi * (n2[None, :] * k1 % TOTAL) / TOTAL for k1 in (pairs, other)]
+    turn = np.stack([np.cos(turns[0]), np.sin(turns[0]), np.cos(turns[1]), np.sin(turns[1])], axis=-1)
+    turn = lax.dynamic_index_in_dim(jnp.asarray(turn.astype(np.float32)), d, 0, keepdims=False)
+    forward = outer_table()
+    tables = []
+    for matrix in (forward, forward.T / TOTAL):
+        matrix = matrix.astype(np.float32)
+        hi = matrix.astype(jnp.bfloat16)
+        tables += [hi, (matrix - hi.astype(np.float32)).astype(jnp.bfloat16)]
+    table = jnp.asarray(np.stack(tables))
+
+    f32 = jnp.float32
+    vmem = pl.BlockSpec(memory_space=pltpu.VMEM)
+    out = pl.pallas_call(
+        fused,
+        out_shape=jax.ShapeDtypeStruct((32, 16, LANES), f32),
+        in_specs=[vmem] * 6,
+        out_specs=vmem,
+        scratch_shapes=[
+            pltpu.VMEM((ROWS, OUTER, LANES), f32),
+            pltpu.VMEM((DEVICES, 2, ROWS, LANES), f32),
+            pltpu.VMEM((DEVICES, 2, ROWS, LANES), f32),
+            pltpu.VMEM((2, LANES, LANES), f32),
+            pltpu.VMEM((2, LANES, LANES), f32),
+            pltpu.VMEM((2, 2, 288, LANES), f32),
+            pltpu.VMEM((2, 2, 272, LANES), f32),
+            pltpu.VMEM((64, 4 * LANES), f32),
+            pltpu.VMEM((2 * LANES, 4 * LANES), jnp.bfloat16),
+            pltpu.VMEM((2 * LANES, 4 * LANES), jnp.bfloat16),
+            pltpu.VMEM((DEVICES, 2, ROWS, LANES), f32),
+            pltpu.VMEM((DEVICES, 2, ROWS, LANES), f32),
+            pltpu.VMEM((ROWS, OUTER, LANES), f32),
+            pltpu.SemaphoreType.DMA((3,)),
+            pltpu.SemaphoreType.DMA((2,)),
+            pltpu.SemaphoreType.DMA((4,)),
+            pltpu.SemaphoreType.DMA((4,)),
+        ],
+        compiler_params=pltpu.CompilerParams(has_side_effects=True, vmem_limit_bytes=32 << 20),
+    )(signal.reshape(32, 16, LANES), resp, gains, base, turn, table)
+    return out.reshape(32, 16 * LANES)
+
+
 def solution(mesh):
+    sizes = dict(mesh.shape)
+    tuned = sizes["tm"] == TM and sizes["chan"] == CHAN
     in_specs = (P("chan", "tm"), P(), P(None, "tm", None, "chan"), P("tm", "chan"))
     out_specs = P("chan", "tm")
     return jax.shard_map(
-        per_device, mesh=mesh, in_specs=in_specs, out_specs=out_specs, check_vma=False
-    )
+        per_device_fused if tuned else per_device, mesh=mesh, in_specs=in_specs, out_specs=out_specs, check_vma=False
+    )

time: 132 us -> 48.4 us (0.37)
  the two profiles are of different devices: /device:TPU:27 before, /device:TPU:0 now
where the time goes in v1:
time: 48.4 us; the launch traced here: 48.1 us
  Pallas kernels  42.4 us (88%)
  local copies, waits for them, and re-layouts  4.84 us (10%)
  other arithmetic  0.81 us (2%)
    pallas_call x1, Pallas kernels, per_device_fused(): pl.pallas_call(fused, out_shape=jax.ShapeDtypeStruct((32, 16, LANES), f32...  42.4 us
    unnamed x6, local copies, waits for them, and re-layouts  1.8 us
    reshape x2, local copies, waits for them, and re-layouts, per_device_fused(): resp = response.reshape(2 * BANDW, 16, 16).transpose(2, 1, 0)  1.05 us

profile of v1, /device:TPU:0, one launch (start us, length us, event | category | flops | bytes accessed | tf_op | source)
XLA Modules:
  0.0 48.1 jit_solution(14779017854842686699)
XLA Ops:
  0.0 0.0 copy-start
  0.0 0.0 copy-start.1
  0.0 0.9 %dynamic-slice_bitcast_fusion.turn = f32[128,4]{1,0:T(8,128)S(1)} fusion(f32[32,128,4]{2,1,0:T(8,128)} %constant.67.clone, s32[]{:T(128)S(6)} %select_n.24), kind=kLoop, calls=%fused_computation.3 | loop fusion | bytes 4100 | tf_op jit(solution)/shard_map/jit(dynamic_index_in_dim)/squeeze | solution.py:405
  0.9 0.9 %reshape.16 = f32[32,16,16]{2,1,0:T(8,128)S(1)} reshape(f32[2,1,16,256]{3,2,1,0:T(8,128)} %param.9) | data formatting | bytes 65536 | tf_op jit(solution)/shard_map/reshape | solution.py:393
  1.8 0.2 copy.9
  1.9 0.7 %fusion.2 = f32[256]{0:T(256)S(1)} fusion(s32[1,256]{1,0:T(1,128)} %param.10), kind=kLoop, calls=%fused_computation.9 | loop fusion | flops 3584 | bytes 2048 | tf_op jit(solution)/shard_map/convert_element_type | solution.py:394
  2.7 0.1 reshape.17
  2.7 0.2 copy.10
  2.9 0.1 select_maximum_fusion.resp
  3.0 1.0 %copy.12 = f32[4,8,16,128]{3,2,1,0:T(8,128)S(1)} copy(f32[4,8,16,128]{3,1,2,0:T(8,128)} %bitcast.19) | data formatting | bytes 524288
  4.0 0.9 %copy.11 = f32[32,256]{0,1:T(8,128)S(1)} copy(f32[32,256]{1,0:T(8,128)} %bitcast.20) | data formatting | bytes 65536 | tf_op jit(solution)/shard_map/reshape | solution.py:396
  4.9 0.0 copy-done
  4.9 0.0 copy-done.1
  4.9 42.4 %shard_map.73 = f32[32,16,128]{2,1,0:T(8,128)S(1)} custom-call(f32[32,16,128]{2,1,0:T(8,128)S(1)} %bitcast.15, f32[16,16,128]{2,1,0:T(8,128)S(1)} %select_maximum_fusion.resp, f32[256,32]{1,0:T(8,128)S(1)} %bitcast.16, f32[2,128,128]{2,1,0:T(8,128)S(1)} %copy-done, f32[128,4]{1,0:T(8,128)S(1)} %dynamic-slice_bitcast_fusion.turn, bf16[4,64,64]{2,1,0:T(8,128)(2,1)S(1)} %copy-done.1), custom_call_target="tpu_custom_call" | custom-call | tf_op jit(solution)/shard_map/pallas_call | solution.py:416
  47.3 0.8 %copy.15 = f32[4,8,16,128]{3,1,2,0:T(8,128)} copy(f32[4,8,16,128]{3,2,1,0:T(8,128)S(1)} %bitcast.14) | data formatting | bytes 524288
Async XLA Ops:
  0.0 4.9 %copy-start = (f32[2,128,128]{2,1,0:T(8,128)S(1)}, f32[2,128,128]{2,1,0:T(8,128)}, u32[]{:S(2)}) copy-start(f32[2,128,128]{2,1,0:T(8,128)} %constant.66.clone.base) | copy-start | bytes 393220
  0.0 4.9 %copy-start.1 = (bf16[4,64,64]{2,1,0:T(8,128)(2,1)S(1)}, bf16[4,64,64]{2,1,0:T(8,128)(2,1)}, u32[]{:S(2)}) copy-start(bf16[4,64,64]{2,1,0:T(8,128)(2,1)} %constant.68.clone.table) | copy-start | bytes 98308

commit v2 on v1

--- a/solution.py
+++ b/solution.py
@@ -214,8 +214,14 @@
     return (t % 2) * 2 + t // 2
 
 
-def fused(signal, resp, band, base, turn, table, out,
-          xin, ybuf, sbuf, rbuf, rt, xp, mv, mm, wh, wl, dbuf, yback, zbuf, rsend, rrecv, send, recv):
+def outer_product(table, value):
+    hi, lo = split_hi_lo(value)
+    return jnp.dot(table.astype(jnp.bfloat16), jnp.concatenate([hi, lo, hi], axis=0), preferred_element_type=jnp.float32)
+
+
+def fused(signal, response, offsets, band_in, base_in, turn_in, table_in, out,
+          base, turn, table, resp, tall, band, xs, xin, ybuf, sbuf, rbuf, rt, xp, mv, mm, wh, wl, vh, vl,
+          dbuf, yback, zbuf, rsend, rrecv, send, recv, own):
     t, g = lax.axis_index("tm"), lax.axis_index("chan")
     d = CHAN // 2 * g + rev(t)
     e = TM * g + t
@@ -228,10 +234,20 @@
     def local(src, dst, sem):
         return pltpu.make_async_copy(src, dst, sem)
 
-    for hop in range(1, TM):
+    for hop in (2, 1, 3):
         to = (t + hop) % TM
-        remote(signal.at[pl.ds(ROWS * to, ROWS)], xin.at[:, pl.ds(16 * t, 16)], 0, (to, g)).start()
-    local(signal.at[pl.ds(ROWS * t, ROWS)], xin.at[:, pl.ds(16 * t, 16)], recv.at[0]).start()
+        remote(signal.at[pl.ds(ROWS * to, ROWS)], xin.at[t], 0, (to, g)).start()
+    local(signal.at[pl.ds(ROWS * t, ROWS)], xin.at[t], recv.at[0]).start()
+    constants = [local(base_in, base, own.at[0]), local(turn_in.at[d], turn, own.at[1]),
+                 local(table_in, table, own.at[2])]
+    for copy in constants:
+        copy.start()
+
+    centered = ((offsets[...] + HALF) % 256 - HALF).astype(jnp.float32)
+    filler = jnp.zeros((LANES - 2 * BANDW - 8, 256), jnp.float32)
+    tall[...] = jnp.concatenate([response[...], jnp.broadcast_to(centered, (8, 256)), filler], axis=0).T
+    for s in range(16):
+        resp[s] = tall[pl.ds(s, 16, stride=16), :]
 
     def send_resp(part, s, block, target):
         return pltpu.make_async_remote_copy(
@@ -256,9 +272,13 @@
             src_ref=resp.at[s_own], dst_ref=rbuf.at[1, pl.ds(16 * g, 16)], send_sem=rsend.at[2],
             recv_sem=rrecv.at[1], device_id=(5 - t, g), device_id_type=pl.DeviceIdType.MESH).start()
 
+    band[...] = jnp.concatenate([band_in[...], jnp.zeros((LANES - 2 * BANDW, 256), jnp.float32)], axis=0).T
+
+    for copy in constants:
+        copy.wait()
     first = d == 0
     for part in range(2):
-        tc, ts = turn[:, 2 * part : 2 * part + 1], turn[:, 2 * part + 1 : 2 * part + 2]
+        tc, ts = turn[2 * part : 2 * part + 1, :], turn[2 * part + 1 : 2 * part + 2, :]
         bc, bs = base[0], base[1]
         tr = tc * bc - ts * bs
         ti = tc * bs + ts * bc
@@ -270,16 +290,20 @@
                       (jnp.where(first, tr, ti), jnp.where(first, ti, -tr)))
         for row in range(2):
             for col in range(2):
-                hi, lo = split_hi_lo(blocks[row][col])
-                where = (slice(LANES * row, LANES * (row + 1)),
-                         slice(LANES * (2 * part + col), LANES * (2 * part + col + 1)))
-                wh[where] = hi
-                wl[where] = lo
+                inner = slice(LANES * row, LANES * (row + 1))
+                outer = slice(LANES * (2 * part + col), LANES * (2 * part + col + 1))
+                vh[outer, inner], vl[outer, inner] = split_hi_lo(blocks[row][col])
+                wh[inner, outer], wl[inner, outer] = split_hi_lo(blocks[row][col].T)
 
     local(xin, xin, recv.at[0]).wait()
+    for b in range(TM):
+        for i in range(16):
+            xs[pl.ds(ROWS * (16 * b + i), ROWS), :] = xin[b, :, LANES * i : LANES * (i + 1)]
     ycols = ybuf.reshape(DEVICES * 2 * ROWS, LANES)
+    taken = jnp.concatenate([xs[pl.ds(c, OUTER, stride=ROWS), :] for c in range(ROWS)], axis=1)
+    result = outer_product(table[0], taken)
     for c in range(ROWS):
-        ycols[pl.ds(c, OUTER, stride=ROWS), :] = dot3((table[0], table[1]), split_hi_lo(xin[c]), ((1,), (0,)))
+        ycols[pl.ds(c, OUTER, stride=ROWS), :] = result[:, LANES * c : LANES * (c + 1)]
 
     def send_pair(hop, carry):
         to = (d + hop) % DEVICES
@@ -317,7 +341,7 @@
                 mv[part, ri, pl.ds(pl.multiple_of(at, 8), 8), :] = got[ri]
         return carry
 
-    lax.fori_loop(0, 34, shift, 0)
+    lax.fori_loop(0, 34, shift, 0, unroll=2)
 
     def chunk(step, carry):
         top = 64 * ((step + g // 2) % 4)
@@ -342,7 +366,7 @@
             return inner
 
         lax.fori_loop(0, 8, mix, 0)
-        back = dot3(split_hi_lo(mm[...]), (wh[...], wl[...]), ((1,), (1,)))
+        back = dot3(split_hi_lo(mm[...]), (vh[...], vl[...]), ((1,), (0,)))
         e0 = top // 8
         for ri in range(2):
             dbuf[pl.ds(e0, 8), ri] = back[:, LANES * ri : LANES * (ri + 1)].reshape(8, 8, LANES)
@@ -367,12 +391,17 @@
 
     local(yback, yback, recv.at[2]).wait()
     bcols = yback.reshape(DEVICES * 2 * ROWS, LANES)
+    taken = jnp.concatenate([bcols[pl.ds(c, OUTER, stride=ROWS), :] for c in range(ROWS)], axis=1)
+    result = outer_product(table[1], taken)
     for c in range(ROWS):
-        zbuf[c] = dot3((table[2], table[3]), split_hi_lo(bcols[pl.ds(c, OUTER, stride=ROWS), :]), ((1,), (0,)))
-    for hop in range(1, TM):
+        xs[pl.ds(c, OUTER, stride=ROWS), :] = result[:, LANES * c : LANES * (c + 1)]
+    for b in range(TM):
+        for i in range(16):
+            zbuf[b, :, LANES * i : LANES * (i + 1)] = xs[pl.ds(ROWS * (16 * b + i), ROWS), :]
+    for hop in (2, 1, 3):
         to = (t + hop) % TM
-        remote(zbuf.at[:, pl.ds(16 * to, 16)], out.at[pl.ds(ROWS * t, ROWS)], 3, (to, g)).start()
-    local(zbuf.at[:, pl.ds(16 * t, 16)], out.at[pl.ds(ROWS * t, ROWS)], recv.at[3]).start()
+        remote(zbuf.at[to], out.at[pl.ds(ROWS * t, ROWS)], 3, (to, g)).start()
+    local(zbuf.at[t], out.at[pl.ds(ROWS * t, ROWS)], recv.at[3]).start()
     local(out, out, recv.at[3]).wait()
 
     for k in (0, 3):
@@ -388,38 +417,40 @@
 
 
 def per_device_fused(signal, band, response, offsets):
-    t, g = lax.axis_index("tm"), lax.axis_index("chan")
-    d = CHAN // 2 * g + rev(t)
-    resp = response.reshape(2 * BANDW, 16, 16).transpose(2, 1, 0)
-    centered = ((offsets + HALF) % 256 - HALF).astype(jnp.float32).reshape(1, 16, 16).transpose(2, 1, 0)
-    resp = jnp.pad(jnp.concatenate([resp, centered], axis=2), ((0, 0), (0, 0), (0, LANES - 2 * BANDW - 1)))
-    gains = band.reshape(2 * BANDW, 256).T
-
     n2 = np.arange(LANES)
     angle = -2 * np.pi * (n2[:, None] * n2[None, :] % LANES) / LANES
     base = jnp.asarray(np.stack([np.cos(angle), np.sin(angle)]).astype(np.float32))
     pairs = np.arange(DEVICES)[:, None]
     other = np.where(pairs == 0, DEVICES, OUTER - pairs)
     turns = [-2 * np.pi * (n2[None, :] * k1 % TOTAL) / TOTAL for k1 in (pairs, other)]
-    turn = np.stack([np.cos(turns[0]), np.sin(turns[0]), np.cos(turns[1]), np.sin(turns[1])], axis=-1)
-    turn = lax.dynamic_index_in_dim(jnp.asarray(turn.astype(np.float32)), d, 0, keepdims=False)
+    rows = [np.cos(turns[0]), np.sin(turns[0]), np.cos(turns[1]), np.sin(turns[1])]
+    turn = jnp.asarray(np.stack(rows * 2, axis=1).astype(np.float32))
     forward = outer_table()
     tables = []
     for matrix in (forward, forward.T / TOTAL):
         matrix = matrix.astype(np.float32)
         hi = matrix.astype(jnp.bfloat16)
-        tables += [hi, (matrix - hi.astype(np.float32)).astype(jnp.bfloat16)]
+        lo = (matrix - hi.astype(np.float32)).astype(jnp.bfloat16)
+        tables.append(np.concatenate([hi, hi, lo], axis=1).astype(np.float32))
     table = jnp.asarray(np.stack(tables))
 
     f32 = jnp.float32
+    hbm = pl.BlockSpec(memory_space=pl.ANY)
     vmem = pl.BlockSpec(memory_space=pltpu.VMEM)
     out = pl.pallas_call(
         fused,
-        out_shape=jax.ShapeDtypeStruct((32, 16, LANES), f32),
-        in_specs=[vmem] * 6,
-        out_specs=vmem,
+        out_shape=jax.ShapeDtypeStruct((32, 16 * LANES), f32),
+        in_specs=[hbm, vmem, vmem, vmem, hbm, hbm, hbm],
+        out_specs=hbm,
         scratch_shapes=[
-            pltpu.VMEM((ROWS, OUTER, LANES), f32),
+            pltpu.VMEM((2, LANES, LANES), f32),
+            pltpu.VMEM((8, LANES), f32),
+            pltpu.VMEM((2, OUTER, 3 * OUTER), f32),
+            pltpu.VMEM((16, 16, LANES), f32),
+            pltpu.VMEM((2 * LANES, LANES), f32),
+            pltpu.VMEM((2 * LANES, LANES), f32),
+            pltpu.VMEM((OUTER * ROWS, LANES), f32),
+            pltpu.VMEM((TM, ROWS, 16 * LANES), f32),
             pltpu.VMEM((DEVICES, 2, ROWS, LANES), f32),
             pltpu.VMEM((DEVICES, 2, ROWS, LANES), f32),
             pltpu.VMEM((2, LANES, LANES), f32),
@@ -429,17 +460,20 @@
             pltpu.VMEM((64, 4 * LANES), f32),
             pltpu.VMEM((2 * LANES, 4 * LANES), jnp.bfloat16),
             pltpu.VMEM((2 * LANES, 4 * LANES), jnp.bfloat16),
+            pltpu.VMEM((4 * LANES, 2 * LANES), jnp.bfloat16),
+            pltpu.VMEM((4 * LANES, 2 * LANES), jnp.bfloat16),
             pltpu.VMEM((DEVICES, 2, ROWS, LANES), f32),
             pltpu.VMEM((DEVICES, 2, ROWS, LANES), f32),
-            pltpu.VMEM((ROWS, OUTER, LANES), f32),
+            pltpu.VMEM((TM, ROWS, 16 * LANES), f32),
             pltpu.SemaphoreType.DMA((3,)),
             pltpu.SemaphoreType.DMA((2,)),
             pltpu.SemaphoreType.DMA((4,)),
             pltpu.SemaphoreType.DMA((4,)),
+            pltpu.SemaphoreType.DMA((3,)),
         ],
         compiler_params=pltpu.CompilerParams(has_side_effects=True, vmem_limit_bytes=32 << 20),
-    )(signal.reshape(32, 16, LANES), resp, gains, base, turn, table)
-    return out.reshape(32, 16 * LANES)
+    )(signal, response.reshape(2 * BANDW, 256), offsets, band.reshape(2 * BANDW, 256), base, turn, table)
+    return out
 
 
 def solution(mesh):

time: 48.4 us -> 49.2 us (1.017)
  local copies, waits for them, and re-layouts: 4.84 us -> 6.56 us
  other arithmetic: 0.81 us -> 0 us
    unnamed x6 -> x15, local copies, waits for them, and re-layouts: 1.8 us -> 6.56 us
    reshape x5 -> x0, local copies, waits for them, and re-layouts: 2.16 us -> none  [the longest x2 1.05 us: per_device_fused(): resp = response.reshape(2 * BANDW, 16, 16).transpose(2, 1, 0)]
    squeeze x1 -> x0, local copies, waits for them, and re-layouts: 0.88 us -> none  [per_device_fused(): lax.dynamic_index_in_dim(jnp.asarray(turn.astype(np.float32)), d, 0, keep...]
    convert_element_type x1 -> x0, other arithmetic: 0.71 us -> none  [per_device_fused(): ((offsets + HALF) % 256 - HALF).astype(jnp.float32).reshape(1, 16, 16)]
where the time goes in v2:
time: 49.2 us; the launch traced here: 48.9 us
  Pallas kernels  42.3 us (86%)
  local copies, waits for them, and re-layouts  6.56 us (13%)
    pallas_call x1, Pallas kernels, per_device_fused(): pl.pallas_call(fused, out_shape=jax.ShapeDtypeStruct((32, 16 * LANES), f3...  42.3 us
    unnamed x15, local copies, waits for them, and re-layouts  6.56 us

profile of v2, /device:TPU:0, one launch (start us, length us, event | category | flops | bytes accessed | tf_op | source)
XLA Modules:
  0.0 48.9 jit_solution(11318137856498846559)
XLA Ops:
  0.0 0.0 copy-start.6
  0.0 0.7 %copy-done.6 = s32[1,256]{1,0:T(1,128)S(1)} copy-done((s32[1,256]{1,0:T(1,128)S(1)}, s32[1,256]{1,0:T(1,128)}, u32[]{:S(2)}) %copy-start.6) | copy-done | bytes 1048
  0.7 0.0 copy-start
  0.7 0.9 %copy-done = f32[32,2048]{1,0:T(8,128)S(1)} copy-done((f32[32,2048]{1,0:T(8,128)S(1)}, f32[32,2048]{1,0:T(8,128)}, u32[]{:S(2)}) %copy-start) | copy-done | bytes 262168
  1.6 0.0 copy-start.1
  1.6 0.9 %copy-done.1 = f32[2,64,192]{2,1,0:T(8,128)S(1)} copy-done((f32[2,64,192]{2,1,0:T(8,128)S(1)}, f32[2,64,192]{2,1,0:T(8,128)}, u32[]{:S(2)}) %copy-start.1) | copy-done | bytes 98328
  2.5 0.0 copy-start.2
  2.5 0.9 %copy-done.2 = f32[32,8,128]{2,1,0:T(8,128)S(1)} copy-done((f32[32,8,128]{2,1,0:T(8,128)S(1)}, f32[32,8,128]{2,1,0:T(8,128)}, u32[]{:S(2)}) %copy-start.2) | copy-done | bytes 131096
  3.4 0.0 copy-start.3
  3.4 0.9 %copy-done.3 = f32[2,128,128]{2,1,0:T(8,128)S(1)} copy-done((f32[2,128,128]{2,1,0:T(8,128)S(1)}, f32[2,128,128]{2,1,0:T(8,128)}, u32[]{:S(2)}) %copy-start.3) | copy-done | bytes 131096
  4.3 0.0 copy-start.4
  4.3 0.8 %copy-done.4 = f32[2,1,16,256]{3,2,1,0:T(8,128)S(1)} copy-done((f32[2,1,16,256]{3,2,1,0:T(8,128)S(1)}, f32[2,1,16,256]{3,2,1,0:T(8,128)}, u32[]{:S(2)}) %copy-start.4) | copy-done | bytes 32792
  5.1 0.0 copy-start.5
  5.1 0.8 %copy-done.5 = f32[2,16,256]{2,1,0:T(8,128)S(1)} copy-done((f32[2,16,256]{2,1,0:T(8,128)S(1)}, f32[2,16,256]{2,1,0:T(8,128)}, u32[]{:S(2)}) %copy-start.5) | copy-done | bytes 32792
  5.9 42.3 %shard_map.73 = f32[32,2048]{1,0:T(8,128)S(1)} custom-call(f32[32,2048]{1,0:T(8,128)S(1)} %copy-done, f32[32,256]{1,0:T(8,128)S(1)} %bitcast.2, s32[1,256]{1,0:T(1,128)S(1)} %copy-done.6, f32[32,256]{1,0:T(8,128)S(1)} %bitcast.3, f32[2,128,128]{2,1,0:T(8,128)S(1)} %copy-done.3, f32[32,8,128]{2,1,0:T(8,128)S(1)} %copy-done.2, f32[2,64,192]{2,1,0:T(8,128)S(1)} %copy-done.1), custom_call_target="tpu_custom_call" | custom-call | tf_op jit(solution)/shard_map/pallas_call | solution.py:440
  48.2 0.7 %copy.9 = f32[32,2048]{1,0:T(8,128)} copy(f32[32,2048]{1,0:T(8,128)S(1)} %shard_map.73) | data formatting | bytes 524288
Async XLA Ops:
  0.0 0.7 %copy-start.6 = (s32[1,256]{1,0:T(1,128)S(1)}, s32[1,256]{1,0:T(1,128)}, u32[]{:S(2)}) copy-start(s32[1,256]{1,0:T(1,128)} %offsets.1) | copy-start | bytes 3076
  0.7 0.9 %copy-start = (f32[32,2048]{1,0:T(8,128)S(1)}, f32[32,2048]{1,0:T(8,128)}, u32[]{:S(2)}) copy-start(f32[32,2048]{1,0:T(8,128)} %signal.1) | copy-start | bytes 786436
  1.6 0.9 %copy-start.1 = (f32[2,64,192]{2,1,0:T(8,128)S(1)}, f32[2,64,192]{2,1,0:T(8,128)}, u32[]{:S(2)}) copy-start(f32[2,64,192]{2,1,0:T(8,128)} %constant.8.clone.table_in) | copy-start | bytes 294916
  2.5 0.9 %copy-start.2 = (f32[32,8,128]{2,1,0:T(8,128)S(1)}, f32[32,8,128]{2,1,0:T(8,128)}, u32[]{:S(2)}) copy-start(f32[32,8,128]{2,1,0:T(8,128)} %constant.7.clone.turn_in) | copy-start | bytes 393220
  3.4 0.9 %copy-start.3 = (f32[2,128,128]{2,1,0:T(8,128)S(1)}, f32[2,128,128]{2,1,0:T(8,128)}, u32[]{:S(2)}) copy-start(f32[2,128,128]{2,1,0:T(8,128)} %constant.6.clone.base_in) | copy-start | bytes 393220
  4.3 0.8 %copy-start.4 = (f32[2,1,16,256]{3,2,1,0:T(8,128)S(1)}, f32[2,1,16,256]{3,2,1,0:T(8,128)}, u32[]{:S(2)}) copy-start(f32[2,1,16,256]{3,2,1,0:T(8,128)} %param.9) | copy-start | bytes 98308
  5.1 0.8 %copy-start.5 = (f32[2,16,256]{2,1,0:T(8,128)S(1)}, f32[2,16,256]{2,1,0:T(8,128)}, u32[]{:S(2)}) copy-start(f32[2,16,256]{2,1,0:T(8,128)} %param.8) | copy-start | bytes 98308

commit v3 on v2

--- a/solution.py
+++ b/solution.py
@@ -219,8 +219,8 @@
     return jnp.dot(table.astype(jnp.bfloat16), jnp.concatenate([hi, lo, hi], axis=0), preferred_element_type=jnp.float32)
 
 
-def fused(signal, response, offsets, band_in, base_in, turn_in, table_in, out,
-          base, turn, table, resp, tall, band, xs, xin, ybuf, sbuf, rbuf, rt, xp, mv, mm, wh, wl, vh, vl,
+def fused(signal, response_in, offsets_in, band_in, base_in, turn_in, table_in, out,
+          response, offsets, band_rows, base, turn, table, resp, tall, band, xs, xin, ybuf, sbuf, rbuf, rt, xp, mv, mm, wh, wl, vh, vl,
           dbuf, yback, zbuf, rsend, rrecv, send, recv, own):
     t, g = lax.axis_index("tm"), lax.axis_index("chan")
     d = CHAN // 2 * g + rev(t)
@@ -234,15 +234,25 @@
     def local(src, dst, sem):
         return pltpu.make_async_copy(src, dst, sem)
 
+    barrier = pltpu.get_barrier_semaphore()
+    for hop in range(1, TM):
+        pl.semaphore_signal(barrier, inc=1, device_id=((t + hop) % TM, g), device_id_type=pl.DeviceIdType.MESH)
+    for hop in range(1, CHAN):
+        pl.semaphore_signal(barrier, inc=1, device_id=(t, (g + hop) % CHAN), device_id_type=pl.DeviceIdType.MESH)
+    copies = [local(src, dst, own.at[i]) for i, (src, dst) in enumerate((
+        (response_in, response), (offsets_in, offsets), (band_in, band_rows), (base_in, base),
+        (turn_in.at[d], turn), (table_in, table)))]
+    for copy in copies:
+        copy.start()
+    pl.semaphore_wait(barrier, TM + CHAN - 2)
+
     for hop in (2, 1, 3):
         to = (t + hop) % TM
         remote(signal.at[pl.ds(ROWS * to, ROWS)], xin.at[t], 0, (to, g)).start()
     local(signal.at[pl.ds(ROWS * t, ROWS)], xin.at[t], recv.at[0]).start()
-    constants = [local(base_in, base, own.at[0]), local(turn_in.at[d], turn, own.at[1]),
-                 local(table_in, table, own.at[2])]
-    for copy in constants:
-        copy.start()
-
+
+    copies[0].wait()
+    copies[1].wait()
     centered = ((offsets[...] + HALF) % 256 - HALF).astype(jnp.float32)
     filler = jnp.zeros((LANES - 2 * BANDW - 8, 256), jnp.float32)
     tall[...] = jnp.concatenate([response[...], jnp.broadcast_to(centered, (8, 256)), filler], axis=0).T
@@ -260,21 +270,21 @@
     for hop in range(1, CHAN):
         to = (g + hop) % CHAN
         send_resp(0, to, g, (t, to)).start()
-        send_resp(1, jnp.where(t == 0, (8 - to) % 8, 7 - to) + 8, g, (t_b, to)).start()
+
+    def send_b():
+        for hop in range(1, CHAN):
+            to = (g + hop) % CHAN
+            send_resp(1, jnp.where(t == 0, (8 - to) % 8, 7 - to) + 8, g, (t_b, to)).start()
 
     @pl.when(t < 2)
     def _():
+        send_b()
         local(resp.at[s_own], rbuf.at[1, pl.ds(16 * g, 16)], rrecv.at[1]).start()
 
-    @pl.when(t >= 2)
-    def _():
-        pltpu.make_async_remote_copy(
-            src_ref=resp.at[s_own], dst_ref=rbuf.at[1, pl.ds(16 * g, 16)], send_sem=rsend.at[2],
-            recv_sem=rrecv.at[1], device_id=(5 - t, g), device_id_type=pl.DeviceIdType.MESH).start()
-
-    band[...] = jnp.concatenate([band_in[...], jnp.zeros((LANES - 2 * BANDW, 256), jnp.float32)], axis=0).T
-
-    for copy in constants:
+    copies[2].wait()
+    band[...] = jnp.concatenate([band_rows[...], jnp.zeros((LANES - 2 * BANDW, 256), jnp.float32)], axis=0).T
+
+    for copy in copies[3:]:
         copy.wait()
     first = d == 0
     for part in range(2):
@@ -296,6 +306,14 @@
                 wh[inner, outer], wl[inner, outer] = split_hi_lo(blocks[row][col].T)
 
     local(xin, xin, recv.at[0]).wait()
+
+    @pl.when(t >= 2)
+    def _():
+        send_b()
+        pltpu.make_async_remote_copy(
+            src_ref=resp.at[s_own], dst_ref=rbuf.at[1, pl.ds(16 * g, 16)], send_sem=rsend.at[2],
+            recv_sem=rrecv.at[1], device_id=(5 - t, g), device_id_type=pl.DeviceIdType.MESH).start()
+
     for b in range(TM):
         for i in range(16):
             xs[pl.ds(ROWS * (16 * b + i), ROWS), :] = xin[b, :, LANES * i : LANES * (i + 1)]
@@ -436,13 +454,15 @@
 
     f32 = jnp.float32
     hbm = pl.BlockSpec(memory_space=pl.ANY)
-    vmem = pl.BlockSpec(memory_space=pltpu.VMEM)
     out = pl.pallas_call(
         fused,
         out_shape=jax.ShapeDtypeStruct((32, 16 * LANES), f32),
-        in_specs=[hbm, vmem, vmem, vmem, hbm, hbm, hbm],
+        in_specs=[hbm] * 7,
         out_specs=hbm,
         scratch_shapes=[
+            pltpu.VMEM((2 * BANDW, 256), f32),
+            pltpu.VMEM((1, 256), jnp.int32),
+            pltpu.VMEM((2 * BANDW, 256), f32),
             pltpu.VMEM((2, LANES, LANES), f32),
             pltpu.VMEM((8, LANES), f32),
             pltpu.VMEM((2, OUTER, 3 * OUTER), f32),
@@ -469,9 +489,9 @@
             pltpu.SemaphoreType.DMA((2,)),
             pltpu.SemaphoreType.DMA((4,)),
             pltpu.SemaphoreType.DMA((4,)),
-            pltpu.SemaphoreType.DMA((3,)),
+            pltpu.SemaphoreType.DMA((6,)),
         ],
-        compiler_params=pltpu.CompilerParams(has_side_effects=True, vmem_limit_bytes=32 << 20),
+        compiler_params=pltpu.CompilerParams(collective_id=0, has_side_effects=True, vmem_limit_bytes=64 << 20),
     )(signal, response.reshape(2 * BANDW, 256), offsets, band.reshape(2 * BANDW, 256), base, turn, table)
     return out
 

time: 49.2 us -> 39.9 us (0.81)
  local copies, waits for them, and re-layouts: 6.56 us -> 1.67 us
  Pallas kernels: 42.3 us -> 38 us
    unnamed x15 -> x1, local copies, waits for them, and re-layouts: 6.56 us -> 1.67 us
    pallas_call x1, Pallas kernels: 42.3 us -> 38 us  [per_device_fused(): pl.pallas_call(fused, out_shape=jax.ShapeDtypeStruct((32, 16 * LANES), f3...]
where the time goes in v3:
time: 39.9 us; the launch traced here: 39.7 us
  Pallas kernels  38 us (95%)
  local copies, waits for them, and re-layouts  1.67 us (4%)
    pallas_call x1, Pallas kernels, per_device_fused(): pl.pallas_call(fused, out_shape=jax.ShapeDtypeStruct((32, 16 * LANES), f3...  38 us
    unnamed x1, local copies, waits for them, and re-layouts  1.67 us

profile of v3, /device:TPU:0, one launch (start us, length us, event | category | flops | bytes accessed | tf_op | source)
XLA Modules:
  0.0 39.7 jit_solution(8805717169604577602)
XLA Ops:
  0.0 38.0 %shard_map.73 = f32[32,2048]{1,0:T(8,128)} custom-call(f32[32,2048]{1,0:T(8,128)} %signal.1, f32[32,256]{1,0:T(8,128)} %bitcast.2, s32[1,256]{1,0:T(1,128)} %offsets_in.1, f32[32,256]{1,0:T(8,128)} %bitcast.3, f32[2,128,128]{2,1,0:T(8,128)} %constant.6.clone.base_in, f32[32,8,128]{2,1,0:T(8,128)} %constant.7.clone.turn_in, f32[2,64,192]{2,1,0:T(8,128)} %constant.8.clone.table_in), custom_call_target="tpu_custom_call" | custom-call | tf_op jit(solution)/shard_map/pallas_call | solution.py:457
  38.0 1.7 %copy.9 = f32[32,2048]{1,0:T(8,128)} copy(f32[32,2048]{1,0:T(8,128)} %shard_map.73) | data formatting | bytes 524288

commit v4 on v3

--- a/solution.py
+++ b/solution.py
@@ -191,13 +191,11 @@
     return hi, (value - hi.astype(jnp.float32)).astype(jnp.bfloat16)
 
 
-def dot3(left, right, dims):
-    (lh, ll), (rh, rl) = left, right
-
-    def one(a, b):
-        return lax.dot_general(a, b, (dims, ((), ())), preferred_element_type=jnp.float32)
-
-    return one(lh, rh) + (one(lh, rl) + one(ll, rh))
+def product(value, table_hi, table_lo):
+    hi, lo = split_hi_lo(value)
+    rows = value.shape[0]
+    both = jnp.dot(jnp.concatenate([hi, lo], axis=0), table_hi[...], preferred_element_type=jnp.float32)
+    return both[:rows] + (both[rows:] + jnp.dot(hi, table_lo[...], preferred_element_type=jnp.float32))
 
 
 def outer_table():
@@ -221,7 +219,7 @@
 
 def fused(signal, response_in, offsets_in, band_in, base_in, turn_in, table_in, out,
           response, offsets, band_rows, base, turn, table, resp, tall, band, xs, xin, ybuf, sbuf, rbuf, rt, xp, mv, mm, wh, wl, vh, vl,
-          dbuf, yback, zbuf, rsend, rrecv, send, recv, own):
+          dbuf, yback, zbuf, rsend, rrecv, send, recv, own, arrive):
     t, g = lax.axis_index("tm"), lax.axis_index("chan")
     d = CHAN // 2 * g + rev(t)
     e = TM * g + t
@@ -323,28 +321,32 @@
     for c in range(ROWS):
         ycols[pl.ds(c, OUTER, stride=ROWS), :] = result[:, LANES * c : LANES * (c + 1)]
 
+    line = g // 2
+
     def send_pair(hop, carry):
-        to = (d + hop) % DEVICES
-        remote(ybuf.at[to], sbuf.at[e], 1, (rev(to % 4), to // 4)).start()
+        to = 8 * ((line + 4 - hop // 8) % 4) + (d + hop) % 8
+        pltpu.make_async_remote_copy(
+            src_ref=ybuf.at[to], dst_ref=sbuf.at[e], send_sem=send.at[1], recv_sem=arrive.at[line],
+            device_id=(rev(to % 4), to // 4), device_id_type=pl.DeviceIdType.MESH).start()
         return carry
 
+    local(ybuf.at[d], sbuf.at[e], arrive.at[line]).start()
     lax.fori_loop(1, DEVICES, send_pair, 0)
-    local(ybuf.at[d], sbuf.at[e], recv.at[1]).start()
 
     for part in range(2):
         local(rbuf.at[part], rbuf.at[part], rrecv.at[part]).wait()
         rt[part] = rbuf[part].T
 
-    local(sbuf, sbuf, recv.at[1]).wait()
-    rows = jnp.concatenate([sbuf[:, 0].reshape(256, LANES), sbuf[:, 1].reshape(256, LANES)], axis=1)
-    spec = dot3(split_hi_lo(rows), (wh[...], wl[...]), ((1,), (0,)))
-    for part in range(2):
-        for ri in range(2):
-            at = LANES * (2 * part + ri)
-            piece = spec[:, at : at + LANES]
-            xp[part, ri, 8:264] = piece
-            xp[part, ri, 0:8] = piece[248:256]
-            xp[part, ri, 264:288] = piece[0:24]
+    def ingest(i):
+        q = (line + i) % 4
+        eight = sbuf.at[pl.ds(8 * q, 8)]
+        local(eight, eight, arrive.at[q]).wait()
+        rows = jnp.concatenate([eight[:, 0].reshape(64, LANES), eight[:, 1].reshape(64, LANES)], axis=1)
+        spec = product(rows, wh, wl)
+        for part in range(2):
+            for ri in range(2):
+                at = LANES * (2 * part + ri)
+                xp[part, ri, pl.ds(pl.multiple_of(64 * i, 64), 64), :] = spec[:, at : at + LANES]
 
     def shift(i, carry):
         at = 8 * i
@@ -354,19 +356,27 @@
             for o in range(-HALF, HALF + 1):
                 hit = off == float(o)
                 for ri in range(2):
-                    got[ri] = jnp.where(hit, xp[part, ri, pl.ds(at + 8 + o, 8), :], got[ri])
+                    got[ri] = jnp.where(hit, xp[part, ri, pl.ds(at + o, 8), :], got[ri])
             for ri in range(2):
                 mv[part, ri, pl.ds(pl.multiple_of(at, 8), 8), :] = got[ri]
         return carry
 
-    lax.fori_loop(0, 34, shift, 0, unroll=2)
+    ingest(0)
+    for part in range(2):
+        for ri in range(2):
+            xp[part, ri, 256:288] = xp[part, ri, 0:32]
+    lax.fori_loop(1, 3, shift, 0, unroll=2)
 
     def chunk(step, carry):
-        top = 64 * ((step + g // 2) % 4)
+        @pl.when(step < 3)
+        def _():
+            ingest(step + 1)
+
+        lax.fori_loop(0, 8, lambda i, inner: shift(8 * step + 3 + i, inner), 0, unroll=2)
 
         def mix(i, inner):
-            at = pl.multiple_of(top + 8 * i, 8)
-            gains = band[pl.ds(at, 8), :]
+            at = 64 * step + 8 + 8 * i
+            gains = band[pl.ds(pl.multiple_of((64 * line + at) % 256, 8), 8), :]
             acc = [jnp.zeros((8, LANES), jnp.float32)] * 4
             for j in range(BANDW):
                 br = jnp.broadcast_to(gains[:, j : j + 1], (8, LANES))
@@ -383,22 +393,22 @@
                 mm[pl.ds(pl.multiple_of(8 * i, 8), 8), LANES * q : LANES * (q + 1)] = acc[q]
             return inner
 
-        lax.fori_loop(0, 8, mix, 0)
-        back = dot3(split_hi_lo(mm[...]), (vh[...], vl[...]), ((1,), (0,)))
-        e0 = top // 8
+        lax.fori_loop(0, 8, mix, 0, unroll=2)
+        back = product(mm[...], vh, vl)
         for ri in range(2):
-            dbuf[pl.ds(e0, 8), ri] = back[:, LANES * ri : LANES * (ri + 1)].reshape(8, 8, LANES)
+            dbuf[pl.ds(8 * step, 8), ri] = back[:, LANES * ri : LANES * (ri + 1)].reshape(8, 8, LANES)
 
         def send_back(u, inner):
-            to = e0 + u
+            source = dbuf.at[8 * step + u]
+            to = (8 * line + 8 * step + 1 + u) % DEVICES
 
             @pl.when(to != e)
             def _():
-                remote(dbuf.at[to], yback.at[d], 2, (to % TM, to // TM)).start()
+                remote(source, yback.at[d], 2, (to % TM, to // TM)).start()
 
             @pl.when(to == e)
             def _():
-                local(dbuf.at[to], yback.at[d], recv.at[2]).start()
+                local(source, yback.at[d], recv.at[2]).start()
 
             return inner
 
@@ -476,7 +486,7 @@
             pltpu.VMEM((2, LANES, LANES), f32),
             pltpu.VMEM((2, LANES, LANES), f32),
             pltpu.VMEM((2, 2, 288, LANES), f32),
-            pltpu.VMEM((2, 2, 272, LANES), f32),
+            pltpu.VMEM((2, 2, 280, LANES), f32),
             pltpu.VMEM((64, 4 * LANES), f32),
             pltpu.VMEM((2 * LANES, 4 * LANES), jnp.bfloat16),
             pltpu.VMEM((2 * LANES, 4 * LANES), jnp.bfloat16),
@@ -490,6 +500,7 @@
             pltpu.SemaphoreType.DMA((4,)),
             pltpu.SemaphoreType.DMA((4,)),
             pltpu.SemaphoreType.DMA((6,)),
+            pltpu.SemaphoreType.DMA((4,)),
         ],
         compiler_params=pltpu.CompilerParams(collective_id=0, has_side_effects=True, vmem_limit_bytes=64 << 20),
     )(signal, response.reshape(2 * BANDW, 256), offsets, band.reshape(2 * BANDW, 256), base, turn, table)

time: 39.9 us -> 38.2 us (0.957)
  Pallas kernels: 38 us -> 36.3 us
    pallas_call x1, Pallas kernels: 38 us -> 36.3 us  [per_device_fused(): pl.pallas_call(fused, out_shape=jax.ShapeDtypeStruct((32, 16 * LANES), f3...]
where the time goes in v4:
time: 38.2 us; the launch traced here: 38 us
  Pallas kernels  36.3 us (95%)
  local copies, waits for them, and re-layouts  1.67 us (4%)
    pallas_call x1, Pallas kernels, per_device_fused(): pl.pallas_call(fused, out_shape=jax.ShapeDtypeStruct((32, 16 * LANES), f3...  36.3 us
    unnamed x1, local copies, waits for them, and re-layouts  1.67 us

profile of v4, /device:TPU:0, one launch (start us, length us, event | category | flops | bytes accessed | tf_op | source)
XLA Modules:
  0.0 38.0 jit_solution(129397662898846129)
XLA Ops:
  0.0 36.3 %shard_map.73 = f32[32,2048]{1,0:T(8,128)} custom-call(f32[32,2048]{1,0:T(8,128)} %signal.1, f32[32,256]{1,0:T(8,128)} %bitcast.2, s32[1,256]{1,0:T(1,128)} %offsets_in.1, f32[32,256]{1,0:T(8,128)} %bitcast.3, f32[2,128,128]{2,1,0:T(8,128)} %constant.6.clone.base_in, f32[32,8,128]{2,1,0:T(8,128)} %constant.7.clone.turn_in, f32[2,64,192]{2,1,0:T(8,128)} %constant.8.clone.table_in), custom_call_target="tpu_custom_call" | custom-call | tf_op jit(solution)/shard_map/pallas_call | solution.py:467
  36.4 1.7 %copy.9 = f32[32,2048]{1,0:T(8,128)} copy(f32[32,2048]{1,0:T(8,128)} %shard_map.73) | data formatting | bytes 524288

commit v5 on v4

--- a/solution.py
+++ b/solution.py
@@ -372,7 +372,7 @@
         def _():
             ingest(step + 1)
 
-        lax.fori_loop(0, 8, lambda i, inner: shift(8 * step + 3 + i, inner), 0, unroll=2)
+        lax.fori_loop(0, 8, lambda i, inner: shift(8 * step + 3 + i, inner), 0, unroll=4)
 
         def mix(i, inner):
             at = 64 * step + 8 + 8 * i
@@ -393,7 +393,7 @@
                 mm[pl.ds(pl.multiple_of(8 * i, 8), 8), LANES * q : LANES * (q + 1)] = acc[q]
             return inner
 
-        lax.fori_loop(0, 8, mix, 0, unroll=2)
+        lax.fori_loop(0, 8, mix, 0, unroll=4)
         back = product(mm[...], vh, vl)
         for ri in range(2):
             dbuf[pl.ds(8 * step, 8), ri] = back[:, LANES * ri : LANES * (ri + 1)].reshape(8, 8, LANES)
@@ -502,8 +502,9 @@
             pltpu.SemaphoreType.DMA((6,)),
             pltpu.SemaphoreType.DMA((4,)),
         ],
-        compiler_params=pltpu.CompilerParams(collective_id=0, has_side_effects=True, vmem_limit_bytes=64 << 20),
-    )(signal, response.reshape(2 * BANDW, 256), offsets, band.reshape(2 * BANDW, 256), base, turn, table)
+        compiler_params=pltpu.CompilerParams(collective_id=0, has_side_effects=True, vmem_limit_bytes=40 << 20),
+    )(*(pltpu.with_memory_space_constraint(x, pltpu.HBM) for x in (
+        signal, response.reshape(2 * BANDW, 256), offsets, band.reshape(2 * BANDW, 256), base, turn, table)))
     return out
 
 

time: 38.2 us -> 36.7 us (0.961)
  local copies, waits for them, and re-layouts: 1.67 us -> 0.71 us
  Pallas kernels: 36.3 us -> 35.8 us
    unnamed x1, local copies, waits for them, and re-layouts: 1.67 us -> 0.71 us
    pallas_call x1, Pallas kernels: 36.3 us -> 35.8 us  [per_device_fused(): pl.pallas_call(fused, out_shape=jax.ShapeDtypeStruct((32, 16 * LANES), f3...]
where the time goes in v5:
time: 36.7 us; the launch traced here: 36.5 us
  Pallas kernels  35.8 us (98%)
  local copies, waits for them, and re-layouts  0.71 us (2%)
    pallas_call x1, Pallas kernels, per_device_fused(): pl.pallas_call(fused, out_shape=jax.ShapeDtypeStruct((32, 16 * LANES), f3...  35.8 us

profile of v5, /device:TPU:0, one launch (start us, length us, event | category | flops | bytes accessed | tf_op | source)
XLA Modules:
  0.0 36.5 jit_solution(665637790895256570)
XLA Ops:
  0.0 35.8 %shard_map.73 = f32[32,2048]{1,0:T(8,128)S(1)} custom-call(f32[32,2048]{1,0:T(8,128)} %signal.1, f32[32,256]{1,0:T(8,128)} %bitcast.2, s32[1,256]{1,0:T(1,128)} %offsets_in.1, f32[32,256]{1,0:T(8,128)} %bitcast.3, f32[2,128,128]{2,1,0:T(8,128)} %constant.6.clone.base_in, f32[32,8,128]{2,1,0:T(8,128)} %constant.7.clone.turn_in, ...), custom_call_target="tpu_custom_call" | custom-call | tf_op jit(solution)/shard_map/pallas_call | solution.py:467
  35.8 0.7 %copy.9 = f32[32,2048]{1,0:T(8,128)} copy(f32[32,2048]{1,0:T(8,128)S(1)} %shard_map.73) | data formatting | bytes 524288

commit v6 on v5

--- a/solution.py
+++ b/solution.py
@@ -219,7 +219,7 @@
 
 def fused(signal, response_in, offsets_in, band_in, base_in, turn_in, table_in, out,
           response, offsets, band_rows, base, turn, table, resp, tall, band, xs, xin, ybuf, sbuf, rbuf, rt, xp, mv, mm, wh, wl, vh, vl,
-          dbuf, yback, zbuf, rsend, rrecv, send, recv, own, arrive):
+          dbuf, yback, zbuf, wide, resp_wide, rsend, rrecv, send, recv, own, arrive):
     t, g = lax.axis_index("tm"), lax.axis_index("chan")
     d = CHAN // 2 * g + rev(t)
     e = TM * g + t
@@ -303,6 +303,15 @@
                 vh[outer, inner], vl[outer, inner] = split_hi_lo(blocks[row][col])
                 wh[inner, outer], wl[inner, outer] = split_hi_lo(blocks[row][col].T)
 
+    def spread(i, carry):
+        rows = pl.ds(pl.multiple_of(8 * i, 8), 8)
+        gains = band[rows, :]
+        for j in range(2 * BANDW):
+            wide[j, rows, :] = jnp.broadcast_to(gains[:, j : j + 1], (8, LANES))
+        return carry
+
+    lax.fori_loop(0, 32, spread, 0)
+
     local(xin, xin, recv.at[0]).wait()
 
     @pl.when(t >= 2)
@@ -336,6 +345,8 @@
     for part in range(2):
         local(rbuf.at[part], rbuf.at[part], rrecv.at[part]).wait()
         rt[part] = rbuf[part].T
+        for j in range(2 * BANDW + 1):
+            resp_wide[part, j] = jnp.broadcast_to(rt[part, j : j + 1, :], (8, LANES))
 
     def ingest(i):
         q = (line + i) % 4
@@ -351,7 +362,7 @@
     def shift(i, carry):
         at = 8 * i
         for part in range(2):
-            off = jnp.broadcast_to(rt[part, 32:33, :], (8, LANES))
+            off = resp_wide[part, 2 * BANDW]
             got = [jnp.zeros((8, LANES), jnp.float32)] * 2
             for o in range(-HALF, HALF + 1):
                 hit = off == float(o)
@@ -372,17 +383,16 @@
         def _():
             ingest(step + 1)
 
-        lax.fori_loop(0, 8, lambda i, inner: shift(8 * step + 3 + i, inner), 0, unroll=4)
+        lax.fori_loop(0, 8, lambda i, inner: shift(8 * step + 3 + i, inner), 0, unroll=8)
 
         def mix(i, inner):
             at = 64 * step + 8 + 8 * i
-            gains = band[pl.ds(pl.multiple_of((64 * line + at) % 256, 8), 8), :]
+            gains = pl.ds(pl.multiple_of((64 * line + at) % 256, 8), 8)
             acc = [jnp.zeros((8, LANES), jnp.float32)] * 4
             for j in range(BANDW):
-                br = jnp.broadcast_to(gains[:, j : j + 1], (8, LANES))
-                bi = jnp.broadcast_to(gains[:, BANDW + j : BANDW + j + 1], (8, LANES))
+                br, bi = wide[j, gains, :], wide[BANDW + j, gains, :]
                 for part in range(2):
-                    rr, ri = rt[part, j : j + 1, :], rt[part, BANDW + j : BANDW + j + 1, :]
+                    rr, ri = resp_wide[part, j], resp_wide[part, BANDW + j]
                     cr = br * rr - bi * ri
                     ci = br * ri + bi * rr
                     xr = mv[part, 0, pl.ds(at + j, 8), :]
@@ -393,7 +403,7 @@
                 mm[pl.ds(pl.multiple_of(8 * i, 8), 8), LANES * q : LANES * (q + 1)] = acc[q]
             return inner
 
-        lax.fori_loop(0, 8, mix, 0, unroll=4)
+        lax.fori_loop(0, 8, mix, 0, unroll=8)
         back = product(mm[...], vh, vl)
         for ri in range(2):
             dbuf[pl.ds(8 * step, 8), ri] = back[:, LANES * ri : LANES * (ri + 1)].reshape(8, 8, LANES)
@@ -495,6 +505,8 @@
             pltpu.VMEM((DEVICES, 2, ROWS, LANES), f32),
             pltpu.VMEM((DEVICES, 2, ROWS, LANES), f32),
             pltpu.VMEM((TM, ROWS, 16 * LANES), f32),
+            pltpu.VMEM((2 * BANDW, 256, LANES), f32),
+            pltpu.VMEM((2, 2 * BANDW + 1, 8, LANES), f32),
             pltpu.SemaphoreType.DMA((3,)),
             pltpu.SemaphoreType.DMA((2,)),
             pltpu.SemaphoreType.DMA((4,)),

time: 36.7 us -> 36.8 us (level)
  no operation moved by 1% of the time
where the time goes in v6:
time: 36.8 us; the launch traced here: 36.7 us
  Pallas kernels  36 us (98%)
  local copies, waits for them, and re-layouts  0.71 us (2%)
    pallas_call x1, Pallas kernels, per_device_fused(): pl.pallas_call(fused, out_shape=jax.ShapeDtypeStruct((32, 16 * LANES), f3...  36 us

profile of v6, /device:TPU:0, one launch (start us, length us, event | category | flops | bytes accessed | tf_op | source)
XLA Modules:
  0.0 36.7 jit_solution(9369076461606204276)
XLA Ops:
  0.0 36.0 %shard_map.73 = f32[32,2048]{1,0:T(8,128)S(1)} custom-call(f32[32,2048]{1,0:T(8,128)} %signal.1, f32[32,256]{1,0:T(8,128)} %bitcast.2, s32[1,256]{1,0:T(1,128)} %offsets_in.1, f32[32,256]{1,0:T(8,128)} %bitcast.3, f32[2,128,128]{2,1,0:T(8,128)} %constant.6.clone.base_in, f32[32,8,128]{2,1,0:T(8,128)} %constant.7.clone.turn_in, ...), custom_call_target="tpu_custom_call" | custom-call | tf_op jit(solution)/shard_map/pallas_call | solution.py:477
  36.0 0.7 %copy.9 = f32[32,2048]{1,0:T(8,128)} copy(f32[32,2048]{1,0:T(8,128)S(1)} %shard_map.73) | data formatting | bytes 524288

commit v7 on v6

--- a/solution.py
+++ b/solution.py
@@ -224,9 +224,9 @@
     d = CHAN // 2 * g + rev(t)
     e = TM * g + t
 
-    def remote(src, dst, k, target):
+    def remote(src, dst, k, target, arrival):
         return pltpu.make_async_remote_copy(
-            src_ref=src, dst_ref=dst, send_sem=send.at[k], recv_sem=recv.at[k],
+            src_ref=src, dst_ref=dst, send_sem=send.at[k], recv_sem=recv.at[arrival],
             device_id=target, device_id_type=pl.DeviceIdType.MESH)
 
     def local(src, dst, sem):
@@ -244,10 +244,11 @@
         copy.start()
     pl.semaphore_wait(barrier, TM + CHAN - 2)
 
-    for hop in (2, 1, 3):
-        to = (t + hop) % TM
-        remote(signal.at[pl.ds(ROWS * to, ROWS)], xin.at[t], 0, (to, g)).start()
-    local(signal.at[pl.ds(ROWS * t, ROWS)], xin.at[t], recv.at[0]).start()
+    for h in range(2):
+        for hop in (2, 1, 3):
+            to = (t + hop) % TM
+            remote(signal.at[pl.ds(ROWS * to + 4 * h, 4)], xin.at[t, pl.ds(4 * h, 4)], 0, (to, g), h).start()
+        local(signal.at[pl.ds(ROWS * t + 4 * h, 4)], xin.at[t, pl.ds(4 * h, 4)], recv.at[h]).start()
 
     copies[0].wait()
     copies[1].wait()
@@ -303,6 +304,38 @@
                 vh[outer, inner], vl[outer, inner] = split_hi_lo(blocks[row][col])
                 wh[inner, outer], wl[inner, outer] = split_hi_lo(blocks[row][col].T)
 
+    line = g // 2
+    ycols = ybuf.reshape(DEVICES * 2 * ROWS, LANES)
+    for h in range(2):
+        half = pl.ds(4 * h, 4)
+        local(xin.at[:, half], xin.at[:, half], recv.at[h]).wait()
+        for b in range(TM):
+            for i in range(16):
+                at = ROWS * (16 * b + i) + 4 * h
+                xs[pl.ds(at, 4), :] = xin[b, 4 * h : 4 * h + 4, LANES * i : LANES * (i + 1)]
+        taken = jnp.concatenate([xs[pl.ds(4 * h + c, OUTER, stride=ROWS), :] for c in range(4)], axis=1)
+        result = outer_product(table[0], taken)
+        for c in range(4):
+            ycols[pl.ds(4 * h + c, OUTER, stride=ROWS), :] = result[:, LANES * c : LANES * (c + 1)]
+
+        def send_pair(hop, carry):
+            to = 8 * ((line + 4 - hop // 8) % 4) + (d + hop) % 8
+            pltpu.make_async_remote_copy(
+                src_ref=ybuf.at[to, :, half], dst_ref=sbuf.at[e, :, half], send_sem=send.at[1],
+                recv_sem=arrive.at[line], device_id=(rev(to % 4), to // 4),
+                device_id_type=pl.DeviceIdType.MESH).start()
+            return carry
+
+        local(ybuf.at[d, :, half], sbuf.at[e, :, half], arrive.at[line]).start()
+        lax.fori_loop(1, DEVICES, send_pair, 0)
+
+    @pl.when(t >= 2)
+    def _():
+        send_b()
+        pltpu.make_async_remote_copy(
+            src_ref=resp.at[s_own], dst_ref=rbuf.at[1, pl.ds(16 * g, 16)], send_sem=rsend.at[2],
+            recv_sem=rrecv.at[1], device_id=(5 - t, g), device_id_type=pl.DeviceIdType.MESH).start()
+
     def spread(i, carry):
         rows = pl.ds(pl.multiple_of(8 * i, 8), 8)
         gains = band[rows, :]
@@ -311,36 +344,6 @@
         return carry
 
     lax.fori_loop(0, 32, spread, 0)
-
-    local(xin, xin, recv.at[0]).wait()
-
-    @pl.when(t >= 2)
-    def _():
-        send_b()
-        pltpu.make_async_remote_copy(
-            src_ref=resp.at[s_own], dst_ref=rbuf.at[1, pl.ds(16 * g, 16)], send_sem=rsend.at[2],
-            recv_sem=rrecv.at[1], device_id=(5 - t, g), device_id_type=pl.DeviceIdType.MESH).start()
-
-    for b in range(TM):
-        for i in range(16):
-            xs[pl.ds(ROWS * (16 * b + i), ROWS), :] = xin[b, :, LANES * i : LANES * (i + 1)]
-    ycols = ybuf.reshape(DEVICES * 2 * ROWS, LANES)
-    taken = jnp.concatenate([xs[pl.ds(c, OUTER, stride=ROWS), :] for c in range(ROWS)], axis=1)
-    result = outer_product(table[0], taken)
-    for c in range(ROWS):
-        ycols[pl.ds(c, OUTER, stride=ROWS), :] = result[:, LANES * c : LANES * (c + 1)]
-
-    line = g // 2
-
-    def send_pair(hop, carry):
-        to = 8 * ((line + 4 - hop // 8) % 4) + (d + hop) % 8
-        pltpu.make_async_remote_copy(
-            src_ref=ybuf.at[to], dst_ref=sbuf.at[e], send_sem=send.at[1], recv_sem=arrive.at[line],
-            device_id=(rev(to % 4), to // 4), device_id_type=pl.DeviceIdType.MESH).start()
-        return carry
-
-    local(ybuf.at[d], sbuf.at[e], arrive.at[line]).start()
-    lax.fori_loop(1, DEVICES, send_pair, 0)
 
     for part in range(2):
         local(rbuf.at[part], rbuf.at[part], rrecv.at[part]).wait()
@@ -408,39 +411,53 @@
         for ri in range(2):
             dbuf[pl.ds(8 * step, 8), ri] = back[:, LANES * ri : LANES * (ri + 1)].reshape(8, 8, LANES)
 
-        def send_back(u, inner):
-            source = dbuf.at[8 * step + u]
+        send_back(step, 0)
+
+        @pl.when(step > 0)
+        def _():
+            send_back(step - 1, 1)
+
+        return carry
+
+    def send_back(step, h):
+        half = pl.ds(4 * h, 4)
+
+        def one(u, inner):
+            source, target = dbuf.at[8 * step + u, :, half], yback.at[d, :, half]
             to = (8 * line + 8 * step + 1 + u) % DEVICES
 
             @pl.when(to != e)
             def _():
-                remote(source, yback.at[d], 2, (to % TM, to // TM)).start()
+                remote(source, target, 2, (to % TM, to // TM), 2 + h).start()
 
             @pl.when(to == e)
             def _():
-                local(source, yback.at[d], recv.at[2]).start()
+                local(source, target, recv.at[2 + h]).start()
 
             return inner
 
-        lax.fori_loop(0, 8, send_back, 0)
-        return carry
+        lax.fori_loop(0, 8, one, 0)
 
     lax.fori_loop(0, 4, chunk, 0)
-
-    local(yback, yback, recv.at[2]).wait()
+    send_back(3, 1)
+
     bcols = yback.reshape(DEVICES * 2 * ROWS, LANES)
-    taken = jnp.concatenate([bcols[pl.ds(c, OUTER, stride=ROWS), :] for c in range(ROWS)], axis=1)
-    result = outer_product(table[1], taken)
-    for c in range(ROWS):
-        xs[pl.ds(c, OUTER, stride=ROWS), :] = result[:, LANES * c : LANES * (c + 1)]
-    for b in range(TM):
-        for i in range(16):
-            zbuf[b, :, LANES * i : LANES * (i + 1)] = xs[pl.ds(ROWS * (16 * b + i), ROWS), :]
-    for hop in (2, 1, 3):
-        to = (t + hop) % TM
-        remote(zbuf.at[to], out.at[pl.ds(ROWS * t, ROWS)], 3, (to, g)).start()
-    local(zbuf.at[t], out.at[pl.ds(ROWS * t, ROWS)], recv.at[3]).start()
-    local(out, out, recv.at[3]).wait()
+    for h in range(2):
+        half = pl.ds(4 * h, 4)
+        local(yback.at[:, :, half], yback.at[:, :, half], recv.at[2 + h]).wait()
+        taken = jnp.concatenate([bcols[pl.ds(4 * h + c, OUTER, stride=ROWS), :] for c in range(4)], axis=1)
+        result = outer_product(table[1], taken)
+        for c in range(4):
+            xs[pl.ds(4 * h + c, OUTER, stride=ROWS), :] = result[:, LANES * c : LANES * (c + 1)]
+        for b in range(TM):
+            for i in range(16):
+                at = ROWS * (16 * b + i) + 4 * h
+                zbuf[b, 4 * h : 4 * h + 4, LANES * i : LANES * (i + 1)] = xs[pl.ds(at, 4), :]
+        for hop in (2, 1, 3):
+            to = (t + hop) % TM
+            remote(zbuf.at[to, half], out.at[pl.ds(ROWS * t + 4 * h, 4)], 3, (to, g), 4).start()
+        local(zbuf.at[t, half], out.at[pl.ds(ROWS * t + 4 * h, 4)], recv.at[4]).start()
+    local(out, out, recv.at[4]).wait()
 
     for k in (0, 3):
         local(signal.at[pl.ds(0, 24)], signal.at[pl.ds(0, 24)], send.at[k]).wait()
@@ -510,7 +527,7 @@
             pltpu.SemaphoreType.DMA((3,)),
             pltpu.SemaphoreType.DMA((2,)),
             pltpu.SemaphoreType.DMA((4,)),
-            pltpu.SemaphoreType.DMA((4,)),
+            pltpu.SemaphoreType.DMA((5,)),
             pltpu.SemaphoreType.DMA((6,)),
             pltpu.SemaphoreType.DMA((4,)),
         ],

time: 36.8 us -> 38.8 us (1.054)
  Pallas kernels: 36 us -> 38 us
    pallas_call x1, Pallas kernels: 36 us -> 38 us  [per_device_fused(): pl.pallas_call(fused, out_shape=jax.ShapeDtypeStruct((32, 16 * LANES), f3...]
where the time goes in v7:
time: 38.8 us; the launch traced here: 38.7 us
  Pallas kernels  38 us (98%)
  local copies, waits for them, and re-layouts  0.71 us (2%)
    pallas_call x1, Pallas kernels, per_device_fused(): pl.pallas_call(fused, out_shape=jax.ShapeDtypeStruct((32, 16 * LANES), f3...  38 us

profile of v7, /device:TPU:0, one launch (start us, length us, event | category | flops | bytes accessed | tf_op | source)
XLA Modules:
  0.0 38.7 jit_solution(14045645121394903175)
XLA Ops:
  0.0 38.0 %shard_map.73 = f32[32,2048]{1,0:T(8,128)S(1)} custom-call(f32[32,2048]{1,0:T(8,128)} %signal.1, f32[32,256]{1,0:T(8,128)} %bitcast.2, s32[1,256]{1,0:T(1,128)} %offsets_in.1, f32[32,256]{1,0:T(8,128)} %bitcast.3, f32[2,128,128]{2,1,0:T(8,128)} %constant.6.clone.base_in, f32[32,8,128]{2,1,0:T(8,128)} %constant.7.clone.turn_in, ...), custom_call_target="tpu_custom_call" | custom-call | tf_op jit(solution)/shard_map/pallas_call | solution.py:494
  38.0 0.7 %copy.9 = f32[32,2048]{1,0:T(8,128)} copy(f32[32,2048]{1,0:T(8,128)S(1)} %shard_map.73) | data formatting | bytes 524288

commit v8 on v6

--- a/solution.py
+++ b/solution.py
@@ -223,6 +223,11 @@
     t, g = lax.axis_index("tm"), lax.axis_index("chan")
     d = CHAN // 2 * g + rev(t)
     e = TM * g + t
+    line = g // 2
+    lines = [(line + i) % 4 for i in range(4)]
+    cores = [g - 2 * line, 1 - (g - 2 * line)]
+    times = [(t + i) % TM for i in range(TM)]
+    revs = [rev(i) for i in times]
 
     def remote(src, dst, k, target):
         return pltpu.make_async_remote_copy(
@@ -330,17 +335,17 @@
     for c in range(ROWS):
         ycols[pl.ds(c, OUTER, stride=ROWS), :] = result[:, LANES * c : LANES * (c + 1)]
 
-    line = g // 2
-
-    def send_pair(hop, carry):
-        to = 8 * ((line + 4 - hop // 8) % 4) + (d + hop) % 8
-        pltpu.make_async_remote_copy(
-            src_ref=ybuf.at[to], dst_ref=sbuf.at[e], send_sem=send.at[1], recv_sem=arrive.at[line],
-            device_id=(rev(to % 4), to // 4), device_id_type=pl.DeviceIdType.MESH).start()
-        return carry
-
     local(ybuf.at[d], sbuf.at[e], arrive.at[line]).start()
-    lax.fori_loop(1, DEVICES, send_pair, 0)
+    for back in range(4):
+        for core in cores:
+            to_g = 2 * lines[-back % 4] + core
+            for hop in (2, 1, 3, 0):
+                if back == 0 and core is cores[0] and hop == 0:
+                    continue
+                pltpu.make_async_remote_copy(
+                    src_ref=ybuf.at[4 * to_g + revs[hop]], dst_ref=sbuf.at[e], send_sem=send.at[1],
+                    recv_sem=arrive.at[line], device_id=(times[hop], to_g),
+                    device_id_type=pl.DeviceIdType.MESH).start()
 
     for part in range(2):
         local(rbuf.at[part], rbuf.at[part], rrecv.at[part]).wait()
@@ -383,7 +388,7 @@
         def _():
             ingest(step + 1)
 
-        lax.fori_loop(0, 8, lambda i, inner: shift(8 * step + 3 + i, inner), 0, unroll=8)
+        lax.fori_loop(0, 8, lambda i, inner: shift(8 * step + 3 + i, inner), 0, unroll=4)
 
         def mix(i, inner):
             at = 64 * step + 8 + 8 * i
@@ -403,26 +408,25 @@
                 mm[pl.ds(pl.multiple_of(8 * i, 8), 8), LANES * q : LANES * (q + 1)] = acc[q]
             return inner
 
-        lax.fori_loop(0, 8, mix, 0, unroll=8)
+        lax.fori_loop(0, 8, mix, 0, unroll=4)
         back = product(mm[...], vh, vl)
         for ri in range(2):
             dbuf[pl.ds(8 * step, 8), ri] = back[:, LANES * ri : LANES * (ri + 1)].reshape(8, 8, LANES)
 
-        def send_back(u, inner):
+        here, after = 2 * ((line + step) % 4), 2 * ((line + step + 1) % 4)
+        for u in range(8):
             source = dbuf.at[8 * step + u]
-            to = (8 * line + 8 * step + 1 + u) % DEVICES
-
-            @pl.when(to != e)
+            to_t, to_g = (1 + u) % 4, (here, here + 1, after)[(1 + u) // 4]
+            own_block = (to_t == t) & (to_g == g)
+
+            @pl.when(jnp.logical_not(own_block))
             def _():
-                remote(source, yback.at[d], 2, (to % TM, to // TM)).start()
-
-            @pl.when(to == e)
+                remote(source, yback.at[d], 2, (to_t, to_g)).start()
+
+            @pl.when(own_block)
             def _():
                 local(source, yback.at[d], recv.at[2]).start()
 
-            return inner
-
-        lax.fori_loop(0, 8, send_back, 0)
         return carry
 
     lax.fori_loop(0, 4, chunk, 0)

time: 36.8 us -> 35.8 us (0.973)
  Pallas kernels: 36 us -> 35 us
    pallas_call x1, Pallas kernels: 36 us -> 35 us  [per_device_fused(): pl.pallas_call(fused, out_shape=jax.ShapeDtypeStruct((32, 16 * LANES), f3...]
where the time goes in v8:
time: 35.8 us; the launch traced here: 35.7 us
  Pallas kernels  35 us (98%)
  local copies, waits for them, and re-layouts  0.71 us (2%)
    pallas_call x1, Pallas kernels, per_device_fused(): pl.pallas_call(fused, out_shape=jax.ShapeDtypeStruct((32, 16 * LANES), f3...  35 us

profile of v8, /device:TPU:0, one launch (start us, length us, event | category | flops | bytes accessed | tf_op | source)
XLA Modules:
  0.0 35.7 jit_solution(9688278596025718186)
XLA Ops:
  0.0 35.0 %shard_map.73 = f32[32,2048]{1,0:T(8,128)S(1)} custom-call(f32[32,2048]{1,0:T(8,128)} %signal.1, f32[32,256]{1,0:T(8,128)} %bitcast.2, s32[1,256]{1,0:T(1,128)} %offsets_in.1, f32[32,256]{1,0:T(8,128)} %bitcast.3, f32[2,128,128]{2,1,0:T(8,128)} %constant.6.clone.base_in, f32[32,8,128]{2,1,0:T(8,128)} %constant.7.clone.turn_in, ...), custom_call_target="tpu_custom_call" | custom-call | tf_op jit(solution)/shard_map/pallas_call | solution.py:481
  35.0 0.7 %copy.9 = f32[32,2048]{1,0:T(8,128)} copy(f32[32,2048]{1,0:T(8,128)S(1)} %shard_map.73) | data formatting | bytes 524288

commit v9 on v8

--- a/solution.py
+++ b/solution.py
@@ -249,9 +249,10 @@
         copy.start()
     pl.semaphore_wait(barrier, TM + CHAN - 2)
 
-    for hop in (2, 1, 3):
-        to = (t + hop) % TM
-        remote(signal.at[pl.ds(ROWS * to, ROWS)], xin.at[t], 0, (to, g)).start()
+    for part in (slice(0, 1024), slice(1024, 2048)):
+        for hop in (2, 1, 3):
+            to = times[hop]
+            remote(signal.at[pl.ds(ROWS * to, ROWS), part], xin.at[t, :, part], 0, (to, g)).start()
     local(signal.at[pl.ds(ROWS * t, ROWS)], xin.at[t], recv.at[0]).start()
 
     copies[0].wait()
@@ -308,23 +309,7 @@
                 vh[outer, inner], vl[outer, inner] = split_hi_lo(blocks[row][col])
                 wh[inner, outer], wl[inner, outer] = split_hi_lo(blocks[row][col].T)
 
-    def spread(i, carry):
-        rows = pl.ds(pl.multiple_of(8 * i, 8), 8)
-        gains = band[rows, :]
-        for j in range(2 * BANDW):
-            wide[j, rows, :] = jnp.broadcast_to(gains[:, j : j + 1], (8, LANES))
-        return carry
-
-    lax.fori_loop(0, 32, spread, 0)
-
     local(xin, xin, recv.at[0]).wait()
-
-    @pl.when(t >= 2)
-    def _():
-        send_b()
-        pltpu.make_async_remote_copy(
-            src_ref=resp.at[s_own], dst_ref=rbuf.at[1, pl.ds(16 * g, 16)], send_sem=rsend.at[2],
-            recv_sem=rrecv.at[1], device_id=(5 - t, g), device_id_type=pl.DeviceIdType.MESH).start()
 
     for b in range(TM):
         for i in range(16):
@@ -346,6 +331,22 @@
                     src_ref=ybuf.at[4 * to_g + revs[hop]], dst_ref=sbuf.at[e], send_sem=send.at[1],
                     recv_sem=arrive.at[line], device_id=(times[hop], to_g),
                     device_id_type=pl.DeviceIdType.MESH).start()
+
+    @pl.when(t >= 2)
+    def _():
+        send_b()
+        pltpu.make_async_remote_copy(
+            src_ref=resp.at[s_own], dst_ref=rbuf.at[1, pl.ds(16 * g, 16)], send_sem=rsend.at[2],
+            recv_sem=rrecv.at[1], device_id=(5 - t, g), device_id_type=pl.DeviceIdType.MESH).start()
+
+    def spread(i, carry):
+        rows = pl.ds(pl.multiple_of(8 * i, 8), 8)
+        gains = band[rows, :]
+        for j in range(2 * BANDW):
+            wide[j, rows, :] = jnp.broadcast_to(gains[:, j : j + 1], (8, LANES))
+        return carry
+
+    lax.fori_loop(0, 32, spread, 0)
 
     for part in range(2):
         local(rbuf.at[part], rbuf.at[part], rrecv.at[part]).wait()
@@ -440,9 +441,10 @@
     for b in range(TM):
         for i in range(16):
             zbuf[b, :, LANES * i : LANES * (i + 1)] = xs[pl.ds(ROWS * (16 * b + i), ROWS), :]
-    for hop in (2, 1, 3):
-        to = (t + hop) % TM
-        remote(zbuf.at[to], out.at[pl.ds(ROWS * t, ROWS)], 3, (to, g)).start()
+    for part in (slice(0, 1024), slice(1024, 2048)):
+        for hop in (2, 1, 3):
+            to = times[hop]
+            remote(zbuf.at[to, :, part], out.at[pl.ds(ROWS * t, ROWS), part], 3, (to, g)).start()
     local(zbuf.at[t], out.at[pl.ds(ROWS * t, ROWS)], recv.at[3]).start()
     local(out, out, recv.at[3]).wait()
 

time: 35.8 us -> 36.8 us (1.028)
  Pallas kernels: 35 us -> 35.9 us
    pallas_call x1, Pallas kernels: 35 us -> 35.9 us  [per_device_fused(): pl.pallas_call(fused, out_shape=jax.ShapeDtypeStruct((32, 16 * LANES), f3...]
where the time goes in v9:
time: 36.8 us; the launch traced here: 36.6 us
  Pallas kernels  35.9 us (98%)
  local copies, waits for them, and re-layouts  0.71 us (2%)
    pallas_call x1, Pallas kernels, per_device_fused(): pl.pallas_call(fused, out_shape=jax.ShapeDtypeStruct((32, 16 * LANES), f3...  35.9 us

profile of v9, /device:TPU:0, one launch (start us, length us, event | category | flops | bytes accessed | tf_op | source)
XLA Modules:
  0.0 36.6 jit_solution(5608859102547033198)
XLA Ops:
  0.0 35.9 %shard_map.73 = f32[32,2048]{1,0:T(8,128)S(1)} custom-call(f32[32,2048]{1,0:T(8,128)} %signal.1, f32[32,256]{1,0:T(8,128)} %bitcast.2, s32[1,256]{1,0:T(1,128)} %offsets_in.1, f32[32,256]{1,0:T(8,128)} %bitcast.3, f32[2,128,128]{2,1,0:T(8,128)} %constant.6.clone.base_in, f32[32,8,128]{2,1,0:T(8,128)} %constant.7.clone.turn_in, ...), custom_call_target="tpu_custom_call" | custom-call | tf_op jit(solution)/shard_map/pallas_call | solution.py:483
  35.9 0.7 %copy.9 = f32[32,2048]{1,0:T(8,128)} copy(f32[32,2048]{1,0:T(8,128)S(1)} %shard_map.73) | data formatting | bytes 524288

commit v10 on v8

--- a/solution.py
+++ b/solution.py
@@ -242,12 +242,25 @@
         pl.semaphore_signal(barrier, inc=1, device_id=((t + hop) % TM, g), device_id_type=pl.DeviceIdType.MESH)
     for hop in range(1, CHAN):
         pl.semaphore_signal(barrier, inc=1, device_id=(t, (g + hop) % CHAN), device_id_type=pl.DeviceIdType.MESH)
+
+    @pl.when(t >= 2)
+    def _():
+        for hop in range(1, CHAN):
+            pl.semaphore_signal(
+                barrier, inc=1, device_id=(5 - t, (g + hop) % CHAN), device_id_type=pl.DeviceIdType.MESH)
+
     copies = [local(src, dst, own.at[i]) for i, (src, dst) in enumerate((
         (response_in, response), (offsets_in, offsets), (band_in, band_rows), (base_in, base),
         (turn_in.at[d], turn), (table_in, table)))]
     for copy in copies:
         copy.start()
-    pl.semaphore_wait(barrier, TM + CHAN - 2)
+    @pl.when(t < 2)
+    def _():
+        pl.semaphore_wait(barrier, TM + CHAN - 2)
+
+    @pl.when(t >= 2)
+    def _():
+        pl.semaphore_wait(barrier, TM + 2 * CHAN - 3)
 
     for hop in (2, 1, 3):
         to = (t + hop) % TM
@@ -283,6 +296,13 @@
     def _():
         send_b()
         local(resp.at[s_own], rbuf.at[1, pl.ds(16 * g, 16)], rrecv.at[1]).start()
+
+    @pl.when(t >= 2)
+    def _():
+        send_b()
+        pltpu.make_async_remote_copy(
+            src_ref=resp.at[s_own], dst_ref=rbuf.at[1, pl.ds(16 * g, 16)], send_sem=rsend.at[2],
+            recv_sem=rrecv.at[1], device_id=(5 - t, g), device_id_type=pl.DeviceIdType.MESH).start()
 
     copies[2].wait()
     band[...] = jnp.concatenate([band_rows[...], jnp.zeros((LANES - 2 * BANDW, 256), jnp.float32)], axis=0).T
@@ -318,13 +338,6 @@
     lax.fori_loop(0, 32, spread, 0)
 
     local(xin, xin, recv.at[0]).wait()
-
-    @pl.when(t >= 2)
-    def _():
-        send_b()
-        pltpu.make_async_remote_copy(
-            src_ref=resp.at[s_own], dst_ref=rbuf.at[1, pl.ds(16 * g, 16)], send_sem=rsend.at[2],
-            recv_sem=rrecv.at[1], device_id=(5 - t, g), device_id_type=pl.DeviceIdType.MESH).start()
 
     for b in range(TM):
         for i in range(16):

time: 35.8 us -> 36.9 us (1.031)
  Pallas kernels: 35 us -> 36 us
    pallas_call x1, Pallas kernels: 35 us -> 36 us  [per_device_fused(): pl.pallas_call(fused, out_shape=jax.ShapeDtypeStruct((32, 16 * LANES), f3...]
where the time goes in v10:
time: 36.9 us; the launch traced here: 36.7 us
  Pallas kernels  36 us (98%)
  local copies, waits for them, and re-layouts  0.71 us (2%)
    pallas_call x1, Pallas kernels, per_device_fused(): pl.pallas_call(fused, out_shape=jax.ShapeDtypeStruct((32, 16 * LANES), f3...  36 us

profile of v10, /device:TPU:0, one launch (start us, length us, event | category | flops | bytes accessed | tf_op | source)
XLA Modules:
  0.0 36.7 jit_solution(5190603838430781982)
XLA Ops:
  0.0 36.0 %shard_map.73 = f32[32,2048]{1,0:T(8,128)S(1)} custom-call(f32[32,2048]{1,0:T(8,128)} %signal.1, f32[32,256]{1,0:T(8,128)} %bitcast.2, s32[1,256]{1,0:T(1,128)} %offsets_in.1, f32[32,256]{1,0:T(8,128)} %bitcast.3, f32[2,128,128]{2,1,0:T(8,128)} %constant.6.clone.base_in, f32[32,8,128]{2,1,0:T(8,128)} %constant.7.clone.turn_in, ...), custom_call_target="tpu_custom_call" | custom-call | tf_op jit(solution)/shard_map/pallas_call | solution.py:494
  36.0 0.7 %copy.9 = f32[32,2048]{1,0:T(8,128)} copy(f32[32,2048]{1,0:T(8,128)S(1)} %shard_map.73) | data formatting | bytes 524288

commit v11 on v8

--- a/solution.py
+++ b/solution.py
@@ -219,7 +219,7 @@
 
 def fused(signal, response_in, offsets_in, band_in, base_in, turn_in, table_in, out,
           response, offsets, band_rows, base, turn, table, resp, tall, band, xs, xin, ybuf, sbuf, rbuf, rt, xp, mv, mm, wh, wl, vh, vl,
-          dbuf, yback, zbuf, wide, resp_wide, rsend, rrecv, send, recv, own, arrive):
+          dbuf, yback, zbuf, resp_wide, rsend, rrecv, send, recv, own, arrive):
     t, g = lax.axis_index("tm"), lax.axis_index("chan")
     d = CHAN // 2 * g + rev(t)
     e = TM * g + t
@@ -308,15 +308,6 @@
                 vh[outer, inner], vl[outer, inner] = split_hi_lo(blocks[row][col])
                 wh[inner, outer], wl[inner, outer] = split_hi_lo(blocks[row][col].T)
 
-    def spread(i, carry):
-        rows = pl.ds(pl.multiple_of(8 * i, 8), 8)
-        gains = band[rows, :]
-        for j in range(2 * BANDW):
-            wide[j, rows, :] = jnp.broadcast_to(gains[:, j : j + 1], (8, LANES))
-        return carry
-
-    lax.fori_loop(0, 32, spread, 0)
-
     local(xin, xin, recv.at[0]).wait()
 
     @pl.when(t >= 2)
@@ -392,10 +383,11 @@
 
         def mix(i, inner):
             at = 64 * step + 8 + 8 * i
-            gains = pl.ds(pl.multiple_of((64 * line + at) % 256, 8), 8)
+            gains = band[pl.ds(pl.multiple_of((64 * line + at) % 256, 8), 8), :]
             acc = [jnp.zeros((8, LANES), jnp.float32)] * 4
             for j in range(BANDW):
-                br, bi = wide[j, gains, :], wide[BANDW + j, gains, :]
+                br = jnp.broadcast_to(gains[:, j : j + 1], (8, LANES))
+                bi = jnp.broadcast_to(gains[:, BANDW + j : BANDW + j + 1], (8, LANES))
                 for part in range(2):
                     rr, ri = resp_wide[part, j], resp_wide[part, BANDW + j]
                     cr = br * rr - bi * ri
@@ -509,7 +501,6 @@
             pltpu.VMEM((DEVICES, 2, ROWS, LANES), f32),
             pltpu.VMEM((DEVICES, 2, ROWS, LANES), f32),
             pltpu.VMEM((TM, ROWS, 16 * LANES), f32),
-            pltpu.VMEM((2 * BANDW, 256, LANES), f32),
             pltpu.VMEM((2, 2 * BANDW + 1, 8, LANES), f32),
             pltpu.SemaphoreType.DMA((3,)),
             pltpu.SemaphoreType.DMA((2,)),

time: 35.8 us -> 36.3 us (1.014)
  Pallas kernels: 35 us -> 35.4 us
    pallas_call x1, Pallas kernels: 35 us -> 35.4 us  [per_device_fused(): pl.pallas_call(fused, out_shape=jax.ShapeDtypeStruct((32, 16 * LANES), f3...]
where the time goes in v11:
time: 36.3 us; the launch traced here: 36.1 us
  Pallas kernels  35.4 us (98%)
  local copies, waits for them, and re-layouts  0.71 us (2%)
    pallas_call x1, Pallas kernels, per_device_fused(): pl.pallas_call(fused, out_shape=jax.ShapeDtypeStruct((32, 16 * LANES), f3...  35.4 us

profile of v11, /device:TPU:0, one launch (start us, length us, event | category | flops | bytes accessed | tf_op | source)
XLA Modules:
  0.0 36.1 jit_solution(8973663179799163701)
XLA Ops:
  0.0 35.4 %shard_map.73 = f32[32,2048]{1,0:T(8,128)S(1)} custom-call(f32[32,2048]{1,0:T(8,128)} %signal.1, f32[32,256]{1,0:T(8,128)} %bitcast.2, s32[1,256]{1,0:T(1,128)} %offsets_in.1, f32[32,256]{1,0:T(8,128)} %bitcast.3, f32[2,128,128]{2,1,0:T(8,128)} %constant.6.clone.base_in, f32[32,8,128]{2,1,0:T(8,128)} %constant.7.clone.turn_in, ...), custom_call_target="tpu_custom_call" | custom-call | tf_op jit(solution)/shard_map/pallas_call | solution.py:473
  35.4 0.7 %copy.9 = f32[32,2048]{1,0:T(8,128)} copy(f32[32,2048]{1,0:T(8,128)S(1)} %shard_map.73) | data formatting | bytes 524288
